TPU v7x, 256 devices: a whole 4x4x8 slice. The times are simulated.
256 devices in a mesh: leaf: 64 (over z, x, core), tile: 4 (over y).
Axes of the slice: x: 4, y: 4, z: 8, core: 2. Of those that a mesh axis runs over, the one named last changes fastest.
Arguments:
- top_sigma: float32 [2048, 2048], P(None, 'tile'), as said below
- anc_a: int32 [64, 12], P('leaf'), may hold values from 0 to 15, as said below
- u_a: float32 [64, 1536, 512], P('leaf'), may hold values from -0.15625 to 0.15625
- dinv_a: float32 [64, 512, 512], P('leaf', None, 'tile'), as said below
- parent: int32 [64], P('leaf'), may hold values from 0 to 63, as said below
- sel_b: int32 [64, 1, 8], P('leaf'), may hold values from 0 to 11, as said below
- pattern: int32 [64, 1, 12, 4], P('leaf'), may hold values 0 or 1
- u_b: float32 [64, 1, 1536, 512], P('leaf'), may hold values from -0.15625 to 0.15625
- dinv_b: float32 [64, 1, 512, 512], P('leaf', None, None, 'tile'), as said below
Outputs:
- sigma_a: float32 [64, 512, 512], P('leaf', None, 'tile')
- sigma_b: float32 [64, 1, 512, 512], P('leaf', None, None, 'tile')
Inputs may be any that keep to these rules, and one draw needn't show every extreme that they name: parent never falls along the leaves, parent[l] <= l, parent[parent[l]] = parent[l], l - parent[l] < 4, some 4 consecutive leaves share one parent, and the last leaf is its own parent. `anc_a`: each row holds distinct tiles in rising order. `sel_b`: each row holds distinct positions in rising order. `top_sigma`: symmetric. `dinv_a`: each block symmetric. `dinv_b`: each block symmetric.
All inputs are finite; a program needn't handle non-finite values. No bound on the sum of `pattern` on one device may be relied on, other than what follows from the above.
Results may differ from a plain program's by a relative error of at most 0.0001.
Values sent between devices are 32-bit elements; how exact they have to be, the bound alone decides.
No kernel may reach another device: no remote copies, remote signals or barrier semaphores. Data moves between devices by JAX's collectives and lax.ppermute only.
A program may use at most 192 MiB of HBM per device.

v0:
```python
import jax
import jax.numpy as jnp
from jax import lax
from jax.sharding import PartitionSpec as P

TB = 128
WT = 4
TOPT = 16
NA = 12
NB = 8
W = 512
SA = 1536
SB = 1536


precise = lax.Precision.HIGHEST


def entering(part, axis, combine, identity):
    place = lax.axis_index(axis)
    gathered = jax.tree.map(lambda a: lax.all_gather(a, axis), part)
    state = jax.tree.map(lambda a, e: jnp.zeros_like(a) + jnp.asarray(e, a.dtype), part, identity)

    def one(hop, state):
        return combine(
            state, jax.tree.map(lambda a: lax.dynamic_index_in_dim(a, hop, 0, False), gathered)
        )

    return lax.fori_loop(0, place, one, state)


def owner_table(indices, first_tile, tile_count):
    return (indices[..., None] == first_tile + jnp.arange(tile_count)).astype(jnp.float32)


def take_latter(earlier, latter):
    take_new = latter[0] > 0
    return (
        jnp.maximum(earlier[0], latter[0]),
        jnp.where(take_new, latter[1], earlier[1]),
        jnp.where(take_new, latter[2], earlier[2]),
    )


def body(top_sigma, anc_a, u_a, dinv_a, parent, sel_b, pattern, u_b, dinv_b):
    tile_count = lax.axis_size("tile")
    tile_pos = lax.axis_index("tile")
    width_dev = W // tile_count
    top_dev = TOPT // tile_count
    local_top = top_sigma.reshape(TOPT, TB, top_dev * TB)
    ancestors = anc_a[0]
    upper_factor = u_a[0]
    rows_upper = jnp.take(local_top, ancestors, axis=0).reshape(SA, top_dev * TB)
    table_upper = owner_table(ancestors, tile_pos * top_dev, top_dev)
    placed_upper = jnp.einsum(
        "jc,jrw->crw", table_upper, upper_factor.reshape(NA, TB, W), precision=precise
    ).reshape(top_dev * TB, W)
    slice_part = placed_upper
    cross_cols = lax.psum_scatter(
        lax.dot_general(
            slice_part,
            rows_upper,
            (((0,), (1,)), ((), ())),
            precision=precise,
            preferred_element_type=jnp.float32,
        ),
        "tile",
        scatter_dimension=0,
        tiled=True,
    )
    own_block = dinv_a[0] + lax.dot_general(
        upper_factor,
        cross_cols,
        (((0,), (1,)), ((), ())),
        precision=precise,
        preferred_element_type=jnp.float32,
    )
    extended = jnp.concatenate([own_block, -cross_cols.T], axis=0)
    position = lax.axis_index("leaf")
    head_of = parent[0]
    is_head = head_of == position
    flag_bit = jnp.where(is_head, 1, 0).astype(jnp.int32).reshape(1)
    sent_ext = jnp.where(is_head, extended, jnp.zeros_like(extended))
    sent_anc = jnp.where(is_head, ancestors, jnp.zeros_like(ancestors))
    identity = (jnp.zeros((1,), jnp.int32), jnp.zeros_like(extended), jnp.zeros_like(ancestors))
    arrived = entering((flag_bit, sent_ext, sent_anc), "leaf", take_latter, identity)
    parent_ext = jnp.where(is_head, extended, arrived[1])
    parent_anc = jnp.where(is_head, ancestors, arrived[2])
    tile_mask = jnp.repeat(jnp.repeat(pattern[0].astype(jnp.float32), TB, axis=1), TB, axis=2)
    factor = u_b[0] * tile_mask
    lower_count = factor.shape[0]
    chosen_ids = sel_b[0]
    tile_order = jnp.concatenate(
        [jnp.broadcast_to(jnp.arange(WT, dtype=jnp.int32), (lower_count, WT)), WT + chosen_ids],
        axis=1,
    )
    ext_tiles = parent_ext.reshape(WT + NA, TB, width_dev)
    chosen = jnp.take(ext_tiles, tile_order, axis=0).reshape(lower_count, SB, width_dev)
    own_rows = lax.dynamic_slice_in_dim(factor, tile_pos * width_dev, width_dev, 1)
    near_rows = jnp.einsum("bsc,bsw->bcw", chosen, factor, precision=precise)
    far_factor = factor[:, W:, :]
    far_partial = jnp.einsum("bxc,bcw->bxw", chosen[:, W:, :], own_rows, precision=precise)
    far_ids = jnp.take(parent_anc, chosen_ids, axis=0)
    rows_far = jnp.take(local_top, far_ids, axis=0).reshape(lower_count, NB * TB, top_dev * TB)
    table_far = owner_table(far_ids, tile_pos * top_dev, top_dev)
    placed_far = jnp.einsum(
        "bjc,bjrw->bcrw", table_far, far_factor.reshape(lower_count, NB, TB, W), precision=precise
    ).reshape(lower_count, top_dev * TB, W)
    far_partial = far_partial + jnp.einsum("bxk,bkw->bxw", rows_far, placed_far, precision=precise)
    far_full = lax.psum(far_partial, "tile")
    slice_part = near_rows
    near_cols = lax.psum_scatter(
        jnp.einsum("bcj,bcw->jbw", slice_part, own_rows, precision=precise),
        "tile",
        scatter_dimension=0,
        tiled=True,
    )
    far_cols = lax.dynamic_slice_in_dim(far_full, tile_pos * width_dev, width_dev, 2)
    update = near_cols.transpose(1, 2, 0) + jnp.einsum(
        "bxw,bxj->bwj", far_factor, far_cols, precision=precise
    )
    sigma_b = (dinv_b[0] + update)[None]
    return (own_block[None], sigma_b)


def solution(mesh):
    in_specs = (
        P(None, "tile"),
        P("leaf", None),
        P("leaf", None, None),
        P("leaf", None, "tile"),
        P("leaf"),
        P("leaf", None, None),
        P("leaf", None, None, None),
        P("leaf", None, None, None),
        P("leaf", None, None, "tile"),
    )
    out_specs = (P("leaf", None, "tile"), P("leaf", None, None, "tile"))
    return jax.shard_map(body, mesh=mesh, in_specs=in_specs, out_specs=out_specs, check_vma=False)
```

profile of v0, /device:TPU:194, one launch (start us, length us, event | category | flops | bytes accessed | tf_op | source)
XLA Modules:
  0.0 733.8 jit_solution(13871045059824685131)
XLA Ops:
  9.1 3.9 fusion.1
  14.3 4.6 gather_fusion
  21.3 12.2 %fusion.60 = f32[512,1536]{1,0:T(8,128)} fusion(f32[512,512]{1,0:T(8,128)S(1)} %bitcast.160, f32[1536,512]{1,0:T(8,128)S(1)} %bitcast.153), kind=kOutput, calls=%fused_computation.89 | convolution fusion | flops 4831838208 | bytes 7340032 | tf_op jit(solution)/shard_map/dot_general | solution.py:60
  36.0 39.3 %reduce-scatter.3.cloned.1.call-done = f32[128,1536]{1,0:T(8,128)} async-done(((f32[512,1536]{1,0:T(8,128)}), f32[128,1536]{1,0:T(8,128)}) %reduce-scatter.3.cloned.1.call-update) | async-done | bytes 786448 | tf_op jit(solution)/shard_map/reduce_scatter | solution.py:59
  87.6 5.0 broadcast_in_dim.90
  92.7 3.6 bitcast_multiply_fusion
  101.0 17.1 %all-reduce = s32[64]{0:T(128)S(1)} all-reduce(s32[64]{0:T(128)S(1)} %dynamic-update-slice), channel_id=1, replica_groups=mesh['leaf'=64,'tile'=4] {'leaf'}, use_global_device_ids=true, to_apply=%add | all-reduce | flops 64 | bytes 512
  118.1 38.9 %all-gather = s32[64,1,12]{2,1,0:T(1,128)S(1)} all-gather(s32[1,1,12]{2,1,0:T(1,128)S(1)} %fusion.48), channel_id=1, replica_groups=mesh['leaf'=64,'tile'=4] {'leaf'}, dimensions={0}, use_global_device_ids=true | all-gather | bytes 3120 | tf_op jit(solution)/shard_map/all_gather | solution.py:21
  157.1 160.4 %all-gather.3.cloned.1.call-done = f32[64,2048,128]{2,1,0:T(8,128)} async-done(((f32[1,2048,128]{2,1,0:T(8,128)}), f32[64,2048,128]{2,1,0:T(8,128)}) %all-gather.3.cloned.1.call-update) | async-done | bytes 67108880 | tf_op jit(solution)/shard_map/all_gather | solution.py:21
  318.7 222.8 %while.14 = (s32[]{:T(128)}, f32[2048,128]{1,0:T(8,128)}, s32[12]{0:T(128)S(1)}, s32[]{:T(128)}, s32[64,1]{0,1:T(1,128)S(1)}, /*index=5*/f32[64,2048,128]{2,1,0:...) while((s32[]{:T(128)}, f32[2048,128]{1,0:T(8,128)}, s32[12]{0:T(128)S(1)}, s32[]{:T(128)}, ...), condition=%wide.region_2.3_spmd, body=%wide.region_1.2_spmd.sunk | while | flops 262162 | bytes 3146026 | solution.py:29
  323.6 3.3 bitcast_select_fusion.4
  328.1 3.3 bitcast_select_fusion.4
  332.7 3.3 bitcast_select_fusion.4
  341.6 3.3 bitcast_select_fusion.4
  346.1 3.3 bitcast_select_fusion.4
  350.7 3.3 bitcast_select_fusion.4
  359.6 3.3 bitcast_select_fusion.4
  376.9 3.3 bitcast_select_fusion.4
  385.8 3.3 bitcast_select_fusion.4
  390.4 3.3 bitcast_select_fusion.4
  443.7 3.3 bitcast_select_fusion.4
  448.3 3.3 bitcast_select_fusion.4
  492.9 3.3 bitcast_select_fusion.4
  542.2 4.2 gather_fusion.3
  546.4 3.8 fusion.10
  561.1 4.8 fusion.61
  568.7 5.0 add_bitcast_fusion
  573.9 5.0 broadcast_in_dim.93
  580.2 5.1 fusion.3
  589.2 103.5 %all-reduce.3.cloned.1.call-done = f32[1,1024,512]{2,1,0:T(8,128)} async-done(((f32[1,1024,512]{2,1,0:T(8,128)}), f32[1,1024,512]{2,1,0:T(8,128)}) %all-reduce.3.cloned.1.call-update) | async-done | bytes 2097168 | tf_op jit(solution)/shard_map/psum | solution.py:110
  692.6 28.5 %reduce-scatter.5.cloned.1.call-done = f32[128,1,512]{0,2,1:T(8,128)} async-done(((f32[512,1,512]{0,2,1:T(8,128)}), f32[128,1,512]{0,2,1:T(8,128)}) %reduce-scatter.5.cloned.1.call-update) | async-done | bytes 262160 | tf_op jit(solution)/shard_map/reduce_scatter | solution.py:112
  721.2 6.0 fusion.27
  (209 shorter events, 223.1 us)
Async XLA Ops:
  7.2 1.9 copy-start
  7.2 68.1 %reduce-scatter.3.cloned.1.call-start = ((), (), s32[]{:S(2)}) async-start(), calls=%async_computation.2 | async-start | bytes 3932160 | tf_op jit(solution)/shard_map/reduce_scatter | solution.py:59
  18.9 2.4 copy-start.3
  33.5 0.9 copy-start.4
  33.6 284.0 %all-gather.3.cloned.1.call-start = ((), (), s32[]{:S(2)}) async-start(), calls=%async_computation.3 | async-start | bytes 68157440 | tf_op jit(solution)/shard_map/all_gather | solution.py:21
  80.5 3.8 copy-start.6
  84.2 608.4 %all-reduce.3.cloned.1.call-start = ((), (), s32[]{:S(2)}) async-start(), calls=%async_computation.5 | async-start | bytes 4194304 | tf_op jit(solution)/shard_map/psum | solution.py:110
  96.3 1.7 copy-start.1
  98.0 1.5 copy-start.7
  98.0 1.7 copy-start.8
  98.0 20.2 %copy-start.5 = (s32[1,12]{1,0:T(1,128)S(1)}, s32[1,12]{1,0:T(1,128)}, u32[]{:S(2)}) copy-start(s32[1,12]{1,0:T(1,128)} %param.12) | copy-start | bytes 148
  559.2 2.0 copy-start.2
  573.7 147.4 %reduce-scatter.5.cloned.1.call-start = ((), (), s32[]{:S(2)}) async-start(), calls=%async_computation.4 | async-start | bytes 1310720 | tf_op jit(solution)/shard_map/reduce_scatter | solution.py:112
Sparse Core Ops, SparseCore 0:
  33.7 41.5 reduce-scatter.2
  84.3 233.1 all-gather.2
  573.8 118.7 all-reduce.2
  695.2 25.9 reduce-scatter.4
where the time goes:
time: 749 us; the launch traced here: 734 us
  waiting for transfers between devices  332 us (44%)
  other arithmetic  238 us (32%)
  blocking collectives  56 us (7%)
  matrix products  46.8 us (6%)
  local copies, waits for them, and re-layouts  44.5 us (6%)
  between operations  14.8 us (2%)
    all_gather x1, waiting for transfers between devices, entering(): gathered = jax.tree.map(lambda a: lax.all_gather(a, axis), part)  160 us
    select_n x50, other arithmetic, take_latter(): jnp.where(take_new, latter[1], earlier[1])  159 us
    psum x1, waiting for transfers between devices, body(): far_full = lax.psum(far_partial, 'tile')  103 us
    reduce_scatter x1, waiting for transfers between devices, body(): lax.psum_scatter(lax.dot_general(slice_part, rows_upper, (((0,), (1,)), (...  39.3 us
    all_gather x1, blocking collectives, entering(): gathered = jax.tree.map(lambda a: lax.all_gather(a, axis), part)  38.9 us
    select_n x50, other arithmetic, take_latter(): jnp.where(take_new, latter[2], earlier[2])  30.9 us
    gt x50, other arithmetic, take_latter(): take_new = latter[0] > 0  30.8 us
    reduce_scatter x1, waiting for transfers between devices, body(): lax.psum_scatter(jnp.einsum('bcj,bcw->jbw', slice_part, own_rows, precisi...  28.5 us
  transfers between devices with their start and end apart: 4, of which 4 were waited for; matrix products, arithmetic and copies ran while one was open for 4% of the time, Pallas kernels for 0%

commit v1 on v0

v1 whole, which is shorter than its diff:
```python
import functools

import jax
import jax.numpy as jnp
from jax import lax
from jax.experimental import pallas as pl
from jax.experimental.pallas import tpu as pltpu
from jax.sharding import PartitionSpec as P

TB = 128
WT = 4
TOPT = 16
NA = 12
NB = 8
W = 512
SA = 1536
SB = 1536
OWN = 4
HALF = 256
F32 = jnp.float32
BF16 = jnp.bfloat16
VMEM_LIMIT = 48 * 1024 * 1024


def split(x):
    high = x.astype(BF16)
    return high, (x - high.astype(F32)).astype(BF16)


def dot3(a, b, contract):
    def one(u, v):
        return lax.dot_general(u, v, (contract, ((), ())), preferred_element_type=F32)

    return one(a[0], b[0]) + (one(a[0], b[1]) + one(a[1], b[0]))


FIRST = ((0,), (0,))
PLAIN = ((1,), (0,))


def upper_rows_kernel(info, g0, g1, g2, g3, u_ref, x_ref):
    step = pl.program_id(0)
    rows = jnp.concatenate([g0[...], g1[...], g2[...], g3[...]], axis=0)
    part = dot3(split(u_ref[0]), split(rows), FIRST)

    @pl.when(step == 0)
    def _():
        x_ref[...] = part

    @pl.when(step > 0)
    def _():
        x_ref[...] += part

    @pl.when(step == pl.num_programs(0) - 1)
    def _():
        for r in range(OWN):
            @pl.when(info[NA + OWN + r] == 0)
            def _():
                x_ref[:, r * TB:(r + 1) * TB] = jnp.zeros((W, TB), F32)


def upper_rows(info, top, u_a):
    def tile(i):
        return pl.BlockSpec((TB, W), lambda k, info: (info[4 * k + i], 0))

    return pl.pallas_call(
        upper_rows_kernel,
        grid_spec=pltpu.PrefetchScalarGridSpec(
            num_scalar_prefetch=1,
            grid=(3,),
            in_specs=[tile(0), tile(1), tile(2), tile(3), pl.BlockSpec((1, W, W), lambda k, info: (0, k, 0))],
            out_specs=pl.BlockSpec((W, W), lambda k, info: (0, 0)),
        ),
        out_shape=jax.ShapeDtypeStruct((W, W), F32),
        compiler_params=pltpu.CompilerParams(vmem_limit_bytes=VMEM_LIMIT),
        cost_estimate=pl.CostEstimate(flops=6 * SA * W * W, bytes_accessed=7 << 20, transcendentals=0),
        name="upper_rows",
    )(info, top, top, top, top, u_a)


def store_slabs(whole, place, slabs):
    for r in range(OWN):
        start = pl.multiple_of(lax.rem(place + r, OWN) * TB, TB)
        slabs[r][...] = whole[:, pl.ds(start, TB)]


def upper_sum_kernel(info, x_ref, u0, u1, u2, u3, s0, s1, s2, s3, whole):
    tiles = [jnp.where(info[NA + OWN + r] > 0, u[0], 0.0) for r, u in enumerate((u0, u1, u2, u3))]
    whole[...] = dot3(split(x_ref[...]), split(jnp.concatenate(tiles, axis=0)), PLAIN)
    store_slabs(whole, info[NA + 2 * OWN], (s0, s1, s2, s3))


def upper_sum(info, x, u_a):
    def tile(r):
        return pl.BlockSpec((1, TB, W), lambda k, info: (0, info[NA + r], 0))

    slab = pl.BlockSpec((W, TB), lambda k, info: (0, 0))
    return pl.pallas_call(
        upper_sum_kernel,
        grid_spec=pltpu.PrefetchScalarGridSpec(
            num_scalar_prefetch=1,
            grid=(1,),
            in_specs=[pl.BlockSpec((W, W), lambda k, info: (0, 0)), tile(0), tile(1), tile(2), tile(3)],
            out_specs=[slab] * 4,
            scratch_shapes=[pltpu.VMEM((W, W), F32)],
        ),
        out_shape=[jax.ShapeDtypeStruct((W, TB), F32)] * 4,
        compiler_params=pltpu.CompilerParams(vmem_limit_bytes=VMEM_LIMIT),
        cost_estimate=pl.CostEstimate(flops=6 * W * W * W, bytes_accessed=3 << 20, transcendentals=0),
        name="upper_sum",
    )(info, x, u_a, u_a, u_a, u_a)


def lower_prepare_kernel(info, *refs):
    g_refs, (u_ref, v_ref, u1h, u1l, u2h, u2l, e1h, e1l, masked) = refs[:NB], refs[NB:]
    mark = NB + 2 * OWN + 1
    for i in range(WT + NB):
        for j in range(WT):
            rows, cols = slice(i * TB, (i + 1) * TB), slice(j * TB, (j + 1) * TB)
            masked[rows, cols] = u_ref[0, 0, rows, cols] * info[mark + i * WT + j].astype(F32)
    near = masked[:W, :].T
    u1h[...], u1l[...] = split(near)
    start = pl.multiple_of(info[NB + 2 * OWN] * TB, TB)
    e1h[...], e1l[...] = split(masked[pl.ds(start, TB), :])
    for r in range(OWN):
        place = pl.multiple_of(W + info[NB + r] * TB, TB)
        own = jnp.where(info[NB + OWN + r] > 0, masked[pl.ds(place, TB), :], 0.0)
        u2h[r * TB:(r + 1) * TB, :], u2l[r * TB:(r + 1) * TB, :] = split(own)
    far = split(masked[W:, :])
    rows = split(jnp.concatenate([g[...] for g in g_refs], axis=0) * 0.5)
    v_ref[...] = dot3(far, rows, FIRST)


def lower_prepare(info, top, u_b):
    def tile(j):
        return pl.BlockSpec((TB, W), lambda k, info: (info[j], 0))

    def whole(rows, cols):
        return pl.BlockSpec((rows, cols), lambda k, info: (0, 0))

    return pl.pallas_call(
        lower_prepare_kernel,
        grid_spec=pltpu.PrefetchScalarGridSpec(
            num_scalar_prefetch=1,
            grid=(1,),
            in_specs=[tile(j) for j in range(NB)] + [pl.BlockSpec((1, 1, SB, W), lambda k, info: (0, 0, 0, 0))],
            out_specs=[whole(W, W)] * 5 + [whole(TB, W)] * 2,
            scratch_shapes=[pltpu.VMEM((SB, W), F32)],
        ),
        out_shape=[jax.ShapeDtypeStruct((W, W), F32)]
        + [jax.ShapeDtypeStruct((W, W), BF16)] * 4
        + [jax.ShapeDtypeStruct((TB, W), BF16)] * 2,
        compiler_params=pltpu.CompilerParams(vmem_limit_bytes=VMEM_LIMIT),
        cost_estimate=pl.CostEstimate(flops=6 * NB * TB * W * W, bytes_accessed=8 << 20, transcendentals=0),
        name="lower_prepare",
    )(info, *([top] * NB), u_b)


def fetch_parent(info, own, other, near, far, swapped, block, sems):
    core = info[1]
    mine = pl.ds(pl.multiple_of(core * HALF, HALF), HALF)
    rest = pl.ds(pl.multiple_of((1 - core) * HALF, HALF), HALF)

    def two(first, second):
        a = pltpu.make_async_copy(first, block.at[mine, :], sems.at[0])
        b = pltpu.make_async_copy(second, block.at[rest, :], sems.at[1])
        a.start()
        b.start()
        a.wait()
        b.wait()

    @pl.when(info[0] == 0)
    def _():
        two(own.at[mine, :], own.at[rest, :])

    @pl.when(info[0] == 1)
    def _():
        two(other.at[mine, :], other.at[rest, :])

    @pl.when(info[0] == 2)
    def _():
        two(near, swapped)

    @pl.when(info[0] == 3)
    def _():
        two(far, swapped)


def lower_cross_kernel(info, own, other, near, far, swapped, v_ref, u1h, u1l, u2h, u2l, p_ref, block, value, sems):
    fetch_parent(info, own, other, near, far, swapped, block, sems)
    value[...] = v_ref[...] - dot3((u1h[...], u1l[...]), split(block[...]), PLAIN)
    for r in range(OWN):
        @pl.when(info[3 + r] == 0)
        def _():
            value[:, r * TB:(r + 1) * TB] = jnp.zeros((W, TB), F32)
    product = dot3(split(value[...]), (u2h[...], u2l[...]), PLAIN)
    p_ref[...] = product + product.T


def lower_cross(info, five, prepared):
    whole = pl.BlockSpec((W, W), lambda k, info: (0, 0))
    return pl.pallas_call(
        lower_cross_kernel,
        grid_spec=pltpu.PrefetchScalarGridSpec(
            num_scalar_prefetch=1,
            grid=(1,),
            in_specs=[pl.BlockSpec(memory_space=pl.ANY)] * 5 + [whole] * 5,
            out_specs=whole,
            scratch_shapes=[pltpu.VMEM((W, W), F32), pltpu.VMEM((W, W), F32), pltpu.SemaphoreType.DMA((2,))],
        ),
        out_shape=jax.ShapeDtypeStruct((W, W), F32),
        compiler_params=pltpu.CompilerParams(vmem_limit_bytes=VMEM_LIMIT),
        cost_estimate=pl.CostEstimate(flops=12 * W * W * W, bytes_accessed=6 << 20, transcendentals=0),
        name="lower_cross",
    )(info, *five, *prepared)


def lower_sum_kernel(info, own, other, near, far, swapped, p_ref, u1h, u1l, e1h, e1l, s0, s1, s2, s3, block, whole, sems):
    fetch_parent(info, own, other, near, far, swapped, block, sems)
    inner = dot3((u1h[...], u1l[...]), split(block[...]), PLAIN)
    whole[...] = p_ref[...] + dot3(split(inner), (e1h[...], e1l[...]), PLAIN)
    store_slabs(whole, info[2], (s0, s1, s2, s3))


def lower_sum(info, five, p, u1h, u1l, e1h, e1l):
    def whole(rows, cols):
        return pl.BlockSpec((rows, cols), lambda k, info: (0, 0))

    return pl.pallas_call(
        lower_sum_kernel,
        grid_spec=pltpu.PrefetchScalarGridSpec(
            num_scalar_prefetch=1,
            grid=(1,),
            in_specs=[pl.BlockSpec(memory_space=pl.ANY)] * 5 + [whole(W, W)] * 3 + [whole(TB, W)] * 2,
            out_specs=[whole(W, TB)] * 4,
            scratch_shapes=[pltpu.VMEM((W, TB), F32), pltpu.VMEM((W, W), F32), pltpu.SemaphoreType.DMA((2,))],
        ),
        out_shape=[jax.ShapeDtypeStruct((W, TB), F32)] * 4,
        compiler_params=pltpu.CompilerParams(vmem_limit_bytes=VMEM_LIMIT),
        cost_estimate=pl.CostEstimate(flops=12 * W * W * TB, bytes_accessed=5 << 20, transcendentals=0),
        name="lower_sum",
    )(info, *five, p, u1h, u1l, e1h, e1l)


def sum_over_tiles(slabs, base, count):
    ways = [[(i, (i + r) % count) for i in range(count)] for r in range(count)]
    arrived = [lax.ppermute(slabs[r], "tile", ways[r]) for r in (2, 1, 3)]
    return base + ((slabs[0] + arrived[1]) + (arrived[0] + arrived[2]))


def body(top, anc_a, u_a, dinv_a, parent, sel_b, pattern, u_b, dinv_b):
    leaves = lax.axis_size("leaf")
    count = lax.axis_size("tile")
    place = lax.axis_index("tile").astype(jnp.int32)
    leaf = lax.axis_index("leaf").astype(jnp.int32)
    core = leaf % 2
    swap = [(i, i ^ 1) for i in range(leaves)]
    next_chip = [(i, i + 2) for i in range(leaves - 2)]
    chip_after = [(i, i + 4) for i in range(leaves - 4)]
    own_tiles = place * OWN + jnp.arange(OWN, dtype=jnp.int32)

    def places(tiles):
        same = own_tiles[:, None] == tiles[None, :]
        at = jnp.sum(jnp.where(same, jnp.arange(tiles.shape[0], dtype=jnp.int32), 0), axis=1)
        return at, jnp.any(same, axis=1).astype(jnp.int32)

    ancestors = anc_a[0]
    at_a, has_a = places(ancestors)
    info_a = jnp.concatenate([ancestors, at_a, has_a, place[None]])
    x = upper_rows(info_a, top, u_a)

    meta = jnp.concatenate([ancestors, parent, jnp.zeros((3,), jnp.int32)])
    meta = jnp.broadcast_to(jnp.pad(meta, (0, 112))[None], (8, 128))
    x, meta = lax.optimization_barrier((x, meta))
    meta_other = lax.ppermute(meta, "leaf", swap)
    even = core == 0
    meta_odd = jnp.where(even, meta_other, meta)
    meta_even = jnp.where(even, meta, meta_other)
    odd_heads = meta_odd[0, NA] == leaf - core + 1
    head = parent[0]
    back = leaf - head
    code = jnp.where(
        back == 0, 0, jnp.where(even, jnp.where(back == 3, 3, 2), jnp.where(back == 1, 1, 2))
    ).astype(jnp.int32)
    even_back = leaf - core - meta_even[0, NA]
    swap_far = jnp.logical_and(jnp.logical_not(even), even_back == 3)

    def send(block):
        other = lax.ppermute(block, "leaf", swap)
        mine = lax.dynamic_slice_in_dim(block, core * HALF, HALF, 0)
        others = lax.dynamic_slice_in_dim(other, core * HALF, HALF, 0)
        odd = jnp.where(even, others, mine)
        latest = jnp.where(jnp.logical_xor(even, odd_heads), mine, others)
        near = lax.ppermute(latest, "leaf", next_chip)
        far = lax.ppermute(odd, "leaf", chip_after)
        return other, near, far

    def receive(block, sent):
        other, near, far = sent
        swapped = lax.ppermute(jnp.where(swap_far, far, near), "leaf", swap)
        return block, other, near, far, swapped

    sent_x = send(x)
    meta_near = lax.ppermute(jnp.where(odd_heads, meta_odd, meta_even), "leaf", next_chip)
    meta_far = lax.ppermute(meta_odd, "leaf", chip_after)
    parent_anc = jnp.where(
        code == 0, meta, jnp.where(code == 1, meta_other, jnp.where(code == 2, meta_near, meta_far))
    )[0, :NA]

    slabs_a = upper_sum(info_a, x, u_a)
    sigma_a = sum_over_tiles(slabs_a, dinv_a[0], count)
    sent_s = send(sigma_a)

    chosen = sel_b[0, 0]
    far_tiles = jnp.sum(
        jnp.where(chosen[:, None] == jnp.arange(NA, dtype=jnp.int32)[None], parent_anc[None], 0), axis=1
    )
    at_b, has_b = places(far_tiles)
    info_b = jnp.concatenate([far_tiles, at_b, has_b, place[None], pattern.reshape(-1)])
    v, u1h, u1l, u2h, u2l, e1h, e1l = lower_prepare(info_b, top, u_b)

    info_c = jnp.concatenate([jnp.stack([code, core, place]), has_b])
    p = lower_cross(info_c, receive(x, sent_x), (v, u1h, u1l, u2h, u2l))
    slabs_b = lower_sum(info_c, receive(sigma_a, sent_s), p, u1h, u1l, e1h, e1l)
    sigma_b = sum_over_tiles(slabs_b, dinv_b[0, 0], count)
    return sigma_a[None], sigma_b[None, None]


def solution(mesh):
    in_specs = (
        P(None, "tile"),
        P("leaf", None),
        P("leaf", None, None),
        P("leaf", None, "tile"),
        P("leaf"),
        P("leaf", None, None),
        P("leaf", None, None, None),
        P("leaf", None, None, None),
        P("leaf", None, None, "tile"),
    )
    out_specs = (P("leaf", None, "tile"), P("leaf", None, None, "tile"))
    return jax.shard_map(body, mesh=mesh, in_specs=in_specs, out_specs=out_specs, check_vma=False)
```

time: 749 us -> 111 us (0.15); the launches traced: 734 us -> 109 us
  waiting for transfers between devices: 332 us -> 42 us
  other arithmetic: 238 us -> 7.05 us
  blocking collectives: 56 us -> 0 us
  matrix products: 46.8 us -> 0 us
  local copies, waits for them, and re-layouts: 44.5 us -> 5.1 us
  starting transfers between devices: 0.34 us -> 28.2 us
  Pallas kernels: 0 us -> 24 us
  between operations: 14.8 us -> 2.89 us
    select_n x110 -> x7, other arithmetic: 200 us -> 1.44 us  [the longest x2 1.33 us: send(): odd = jnp.where(even, others, mine)]
    all_gather x1 -> x0, waiting for transfers between devices: 160 us -> none  [entering(): gathered = jax.tree.map(lambda a: lax.all_gather(a, axis), part)]
    psum x1 -> x0, waiting for transfers between devices: 103 us -> none  [body(): far_full = lax.psum(far_partial, 'tile')]
    reduce_scatter x2 -> x0, waiting for transfers between devices: 67.9 us -> none  [the longest x1 39.3 us: body(): lax.psum_scatter(lax.dot_general(slice_part, rows_upper, (((0,), (1,)), (...]
    dot_general x9 -> x0, matrix products: 46.8 us -> none  [the longest x1 12.2 us: body(): lax.dot_general(slice_part, rows_upper, (((0,), (1,)), ((), ())), precisi...]
    ppermute x0 -> x17, waiting for transfers between devices: none -> 42 us  [the longest x2 15.7 us: send(): near = lax.ppermute(latest, 'leaf', next_chip)]
    all_gather x1 -> x0, blocking collectives: 38.9 us -> none  [entering(): gathered = jax.tree.map(lambda a: lax.all_gather(a, axis), part)]
    gt x50 -> x0, other arithmetic: 30.8 us -> none  [take_latter(): take_new = latter[0] > 0]
  transfers between devices with their start and end apart: 4 -> 17, of which waited for: 4 -> 6; matrix products, arithmetic and copies ran while one was open for 4% -> 4% of each run, Pallas kernels for 0% -> 13%
where the time goes in v1:
time: 111 us; the launch traced here: 109 us
  waiting for transfers between devices  42 us (38%)
  starting transfers between devices  28.2 us (25%)
  Pallas kernels  24 us (22%)
  other arithmetic  7.05 us (6%)
  local copies, waits for them, and re-layouts  5.1 us (5%)
  between operations  2.89 us (3%)
    ppermute x2, waiting for transfers between devices, send(): near = lax.ppermute(latest, 'leaf', next_chip)  15.7 us
    ppermute x6, waiting for transfers between devices, sum_over_tiles(): arrived = [lax.ppermute(slabs[r], 'tile', ways[r]) for r in (2, 1, 3)]  12.8 us
    ppermute x2, waiting for transfers between devices, send(): far = lax.ppermute(odd, 'leaf', chip_after)  11.6 us
    ppermute x6, starting transfers between devices, sum_over_tiles(): arrived = [lax.ppermute(slabs[r], 'tile', ways[r]) for r in (2, 1, 3)]  9.33 us
    pallas_call x1, Pallas kernels, upper_rows(): pl.pallas_call(upper_rows_kernel, grid_spec=pltpu.PrefetchScalarGridSpec(...  6.52 us
    ppermute x2, starting transfers between devices, send(): near = lax.ppermute(latest, 'leaf', next_chip)  5.93 us
    ppermute x2, starting transfers between devices, send(): far = lax.ppermute(odd, 'leaf', chip_after)  5.93 us
    pallas_call x1, Pallas kernels, lower_prepare(): pl.pallas_call(lower_prepare_kernel, grid_spec=pltpu.PrefetchScalarGridSp...  5.49 us
  transfers between devices with their start and end apart: 17, of which 6 were waited for; matrix products, arithmetic and copies ran while one was open for 4% of the time, Pallas kernels for 13%

profile of v1, /device:TPU:194, one launch (start us, length us, event | category | flops | bytes accessed | tf_op | source)
XLA Modules:
  0.0 109.2 jit_solution(15721112222852195172)
XLA Ops:
  0.6 0.8 compare_reduce_fusion.1
  1.5 0.8 fusion.1
  3.0 0.7 pad_add_fusion.1
  3.7 0.7 pad_add_fusion.info
  4.5 1.9 %copy-done = f32[1,1536,512]{2,1,0:T(8,128)S(1)} copy-done((f32[1,1536,512]{2,1,0:T(8,128)S(1)}, f32[1,1536,512]{2,1,0:T(8,128)}, u32[]{:S(2)}) %copy-start) | copy-done | bytes 3145752
  6.4 6.5 %upper_rows.1.x_ref.own = f32[512,512]{1,0:T(8,128)} custom-call(s32[21]{0:T(128)S(1)} %pad_add_fusion.info, f32[2048,512]{1,0:T(8,128)} %refs_7_.1, f32[2048,512]{1,0:T(8,128)} %refs_7_.1, f32[2048,512]{1,0:T(8,128)} %refs_7_.1, f32[2048,512]{1,0:T(8,128)} %refs_7_.1, f32[1,1536,512]{2,1,0:T(8,128)S(1)} %copy-done), custom_call_target="tpu_custom_call" | custom-call | flops 2415919104 | bytes 7340032 | tf_op jit(solution)/shard_map/upper_rows/pallas_call | solution.py:66
  13.4 1.8 %collective-permute-done.3 = s32[8,128]{1,0:T(8,128)S(1)} collective-permute-done((s32[8,128]{1,0:T(8,128)S(1)}, s32[8,128]{1,0:T(8,128)S(1)}, u32[]{:S(2)}, u32[]{:S(2)}) %collective-permute-start.3) | collective-permute-done | bytes 4128 | tf_op jit(solution)/shard_map/ppermute | solution.py:275
  15.8 4.0 %collective-permute-start.5 = (s32[8,128]{1,0:T(8,128)S(1)}, s32[8,128]{1,0:T(8,128)S(1)}, u32[]{:S(2)}, u32[]{:S(2)}) collective-permute-start(s32[8,128]{1,0:T(8,128)S(1)} %broadcast_select_fusion.4), channel_id=1, source_target_pairs={{0,16},{4,20},{8,24},{12,28},{16,32},{20,36},{24,40},{28,44},{32,4... | collective-permute-start | bytes 12296 | tf_op jit(solution)/shard_map/ppermute | solution.py:305
  20.5 2.2 %collective-permute-start.4 = (s32[8,128]{1,0:T(8,128)S(1)}, s32[8,128]{1,0:T(8,128)S(1)}, u32[]{:S(2)}, u32[]{:S(2)}) collective-permute-start(s32[8,128]{1,0:T(8,128)S(1)} %get-tuple-element.36), channel_id=1, source_target_pairs={{0,8},{4,12},{8,16},{12,20},{16,24},{20,28},{24,32},{28,36},{32,40... | collective-permute-start | bytes 12296 | tf_op jit(solution)/shard_map/ppermute | solution.py:304
  22.7 3.7 %upper_sum.1 = (f32[512,128]{1,0:T(8,128)S(1)}, f32[512,128]{1,0:T(8,128)}, f32[512,128]{1,0:T(8,128)}, f32[512,128]{1,0:T(8,128)S(1)}) custom-call(s32[21]{0:T(128)S(1)} %pad_add_fusion.info, f32[512,512]{1,0:T(8,128)} %upper_rows.1.x_ref.own, f32[1,1536,512]{2,1,0:T(8,128)S(1)} %copy-done.1, f32[1,1536,512]{2,1,0:T(8,128)S(1)} %copy-done.1, ...), custom_call_target="tpu_custom_call" | custom-call | flops 805306368 | bytes 3145728 | tf_op jit(solution)/shard_map/upper_sum/pallas_call | solution.py:98
  26.5 0.7 copy-done.4
  27.2 1.6 %collective-permute-start = (f32[512,128]{1,0:T(8,128)}, f32[512,128]{1,0:T(8,128)S(1)}, u32[]{:S(2)}, u32[]{:S(2)}) collective-permute-start(f32[512,128]{1,0:T(8,128)} %get-tuple-element.21), channel_id=1, source_target_pairs={{0,1},{1,2},{2,3},{3,0},{4,5},{5,6},{6,7},{7,4},{8,9},{9,10},{10,1... | collective-permute-start | bytes 786440 | tf_op jit(solution)/shard_map/ppermute | solution.py:247
  28.8 2.9 %collective-permute-start.1 = (f32[512,128]{1,0:T(8,128)}, f32[512,128]{1,0:T(8,128)S(1)}, u32[]{:S(2)}, u32[]{:S(2)}) collective-permute-start(f32[512,128]{1,0:T(8,128)} %get-tuple-element.22), channel_id=1, source_target_pairs={{0,2},{1,3},{2,0},{3,1},{4,6},{5,7},{6,4},{7,5},{8,10},{9,11},{10,... | collective-permute-start | bytes 786440 | tf_op jit(solution)/shard_map/ppermute | solution.py:247
  31.9 0.6 slice.11
  33.2 1.4 %collective-permute-start.2 = (f32[512,128]{1,0:T(8,128)}, f32[512,128]{1,0:T(8,128)S(1)}, u32[]{:S(2)}, u32[]{:S(2)}) collective-permute-start(f32[512,128]{1,0:T(8,128)} %copy-done.4), channel_id=1, source_target_pairs={{0,3},{1,0},{2,1},{3,2},{4,7},{5,4},{6,5},{7,6},{8,11},{9,8},{10,9... | collective-permute-start | bytes 786440 | tf_op jit(solution)/shard_map/ppermute | solution.py:247
  34.6 1.3 %dynamic-slice_select_fusion = (f32[256,512]{1,0:T(8,128)S(1)}, f32[256,512]{1,0:T(8,128)S(1)}) fusion(f32[512,512]{1,0:T(8,128)} %collective-permute-done.10.other, s32[]{:T(128)S(6)} %select_n.135, f32[512,512]{1,0:T(8,128)} %upper_rows.1.x_ref.own, pred[]{:T(512)S(6)} %eq.74, pred[]{:T(512)S(6)} %xor.4), kind=kLoop, calls=%fused_computation | loop fusion | flops 262144 | bytes 2097158 | tf_op jit(solution)/shard_map/jit(_where)/select_n | solution.py:292
  35.9 4.0 %collective-permute-start.11 = (f32[256,512]{1,0:T(8,128)S(1)}, f32[256,512]{1,0:T(8,128)S(1)}, u32[]{:S(2)}, u32[]{:S(2)}) collective-permute-start(f32[256,512]{1,0:T(8,128)S(1)} %get-tuple-element.39), channel_id=1, source_target_pairs={{0,8},{4,12},{8,16},{12,20},{16,24},{20,28},{24,32},{28,36},{32,40... | collective-permute-start | bytes 1572872 | tf_op jit(solution)/shard_map/ppermute | solution.py:294
  39.9 4.0 %collective-permute-start.12 = (f32[256,512]{1,0:T(8,128)S(1)}, f32[256,512]{1,0:T(8,128)S(1)}, u32[]{:S(2)}, u32[]{:S(2)}) collective-permute-start(f32[256,512]{1,0:T(8,128)S(1)} %get-tuple-element.38), channel_id=1, source_target_pairs={{0,16},{4,20},{8,24},{12,28},{16,32},{20,36},{24,40},{28,44},{32,4... | collective-permute-start | bytes 1572872 | tf_op jit(solution)/shard_map/ppermute | solution.py:295
  44.6 1.0 bitcast_add_fusion.1.own
  45.8 15.7 %collective-permute-done.11.near = f32[256,512]{1,0:T(8,128)S(1)} collective-permute-done((f32[256,512]{1,0:T(8,128)S(1)}, f32[256,512]{1,0:T(8,128)S(1)}, u32[]{:S(2)}, u32[]{:S(2)}) %collective-permute-start.11) | collective-permute-done | bytes 524320 | tf_op jit(solution)/shard_map/ppermute | solution.py:294
  61.5 9.9 %collective-permute-done.12.far = f32[256,512]{1,0:T(8,128)S(1)} collective-permute-done((f32[256,512]{1,0:T(8,128)S(1)}, f32[256,512]{1,0:T(8,128)S(1)}, u32[]{:S(2)}, u32[]{:S(2)}) %collective-permute-start.12) | collective-permute-done | bytes 524320 | tf_op jit(solution)/shard_map/ppermute | solution.py:295
  71.6 1.9 %collective-permute-start.7 = (f32[256,128]{1,0:T(8,128)S(1)}, f32[256,128]{1,0:T(8,128)S(1)}, u32[]{:S(2)}, u32[]{:S(2)}) collective-permute-start(f32[256,128]{1,0:T(8,128)S(1)} %get-tuple-element.41), channel_id=1, source_target_pairs={{0,8},{4,12},{8,16},{12,20},{16,24},{20,28},{24,32},{28,36},{32,40... | collective-permute-start | bytes 393224 | tf_op jit(solution)/shard_map/ppermute | solution.py:294
  73.6 1.9 %collective-permute-start.8 = (f32[256,128]{1,0:T(8,128)S(1)}, f32[256,128]{1,0:T(8,128)S(1)}, u32[]{:S(2)}, u32[]{:S(2)}) collective-permute-start(f32[256,128]{1,0:T(8,128)S(1)} %get-tuple-element.40), channel_id=1, source_target_pairs={{0,16},{4,20},{8,24},{12,28},{16,32},{20,36},{24,40},{28,44},{32,4... | collective-permute-start | bytes 393224 | tf_op jit(solution)/shard_map/ppermute | solution.py:295
  75.5 5.5 %lower_prepare.1 = (f32[512,512]{1,0:T(8,128)S(1)}, bf16[512,512]{1,0:T(8,128)(2,1)S(1)}, bf16[512,512]{1,0:T(8,128)(2,1)S(1)}, bf16[512,512]{1,0:T(8,128)(2,1)S...) custom-call(s32[65]{0:T(128)S(1)} %concatenate.15.info, ...), custom_call_target="tpu_custom_call" | custom-call | flops 1610612736 | bytes 8388608 | tf_op jit(solution)/shard_map/lower_prepare/pallas_call | solution.py:141
  81.0 1.0 copy-done.3
  82.0 1.7 %collective-permute-done.8.far = f32[256,128]{1,0:T(8,128)S(1)} collective-permute-done((f32[256,128]{1,0:T(8,128)S(1)}, f32[256,128]{1,0:T(8,128)S(1)}, u32[]{:S(2)}, u32[]{:S(2)}) %collective-permute-start.8) | collective-permute-done | bytes 131104 | tf_op jit(solution)/shard_map/ppermute | solution.py:295
  83.9 5.4 %lower_cross.1.p_ref = f32[512,512]{1,0:T(8,128)S(1)} custom-call(s32[7]{0:T(128)S(1)} %pad_add_fusion.2.info, f32[512,512]{1,0:T(8,128)} %upper_rows.1.x_ref.own, f32[512,512]{1,0:T(8,128)} %collective-permute-done.10.other, f32[256,512]{1,0:T(8,128)S(1)} %collective-permute-done.11.near, f32[256,512]{1,0:T(8,128)S(1)} %collective-permute-done.12.far, ...), custom_call_target="tpu_custom_call" | custom-call | flops 1610612736 | bytes 6291456 | tf_op jit(solution)/shard_map/lower_cross/pallas_call | solution.py:202
  89.3 2.8 %lower_sum.1 = (f32[512,128]{1,0:T(8,128)S(1)}, f32[512,128]{1,0:T(8,128)S(1)}, f32[512,128]{1,0:T(8,128)S(1)}, f32[512,128]{1,0:T(8,128)S(1)}) custom-call(s32[7]{0:T(128)S(1)} %pad_add_fusion.2.info, f32[512,128]{1,0:T(8,128)S(1)} %bitcast_add_fusion.1.own, f32[512,128]{1,0:T(8,128)S(1)} %collective-permute-done.6.other, ...), custom_call_target="tpu_custom_call" | custom-call | flops 402653184 | bytes 5242880 | tf_op jit(solution)/shard_map/lower_sum/pallas_call | solution.py:229
  92.8 1.5 %collective-permute-start.15 = (f32[512,128]{1,0:T(8,128)S(1)}, f32[512,128]{1,0:T(8,128)S(1)}, u32[]{:S(2)}, u32[]{:S(2)}) collective-permute-start(f32[512,128]{1,0:T(8,128)S(1)} %get-tuple-element.34), channel_id=1, source_target_pairs={{0,2},{1,3},{2,0},{3,1},{4,6},{5,7},{6,4},{7,5},{8,10},{9,11},{10,... | collective-permute-start | bytes 786440 | tf_op jit(solution)/shard_map/ppermute | solution.py:247
  94.3 1.3 %collective-permute-start.16 = (f32[512,128]{1,0:T(8,128)S(1)}, f32[512,128]{1,0:T(8,128)S(1)}, u32[]{:S(2)}, u32[]{:S(2)}) collective-permute-start(f32[512,128]{1,0:T(8,128)S(1)} %get-tuple-element.35), channel_id=1, source_target_pairs={{0,3},{1,0},{2,1},{3,2},{4,7},{5,4},{6,5},{7,6},{8,11},{9,8},{10,9... | collective-permute-start | bytes 786440 | tf_op jit(solution)/shard_map/ppermute | solution.py:247
  95.6 12.2 %collective-permute-done.14 = f32[512,128]{1,0:T(8,128)S(1)} collective-permute-done((f32[512,128]{1,0:T(8,128)S(1)}, f32[512,128]{1,0:T(8,128)S(1)}, u32[]{:S(2)}, u32[]{:S(2)}) %collective-permute-start.14) | collective-permute-done | bytes 262176 | tf_op jit(solution)/shard_map/ppermute | solution.py:247
  108.4 0.8 fusion
  (52 shorter events, 3.8 us)
Async XLA Ops:
  4.5 1.9 %copy-start = (f32[1,1536,512]{2,1,0:T(8,128)S(1)}, f32[1,1536,512]{2,1,0:T(8,128)}, u32[]{:S(2)}) copy-start(f32[1,1536,512]{2,1,0:T(8,128)} %u3.1) | copy-start | bytes 9437188
  6.4 16.4 %copy-start.1 = (f32[1,1536,512]{2,1,0:T(8,128)S(1)}, f32[1,1536,512]{2,1,0:T(8,128)}, u32[]{:S(2)}) copy-start(f32[1,1536,512]{2,1,0:T(8,128)} %u3.1) | copy-start | bytes 9437188
  12.9 21.7 %collective-permute-start.10 = (f32[512,512]{1,0:T(8,128)}, f32[512,512]{1,0:T(8,128)}, u32[]{:S(2)}, u32[]{:S(2)}) collective-permute-start(f32[512,512]{1,0:T(8,128)} %upper_rows.1.x_ref.own), channel_id=1, source_target_pairs={{0,4},{4,0},{8,12},{12,8},{16,20},{20,16},{24,28},{28,24},{32,36},... | collective-permute-start | bytes 3145736 | tf_op jit(solution)/shard_map/ppermute | solution.py:289
  12.9 2.3 %collective-permute-start.3 = (s32[8,128]{1,0:T(8,128)S(1)}, s32[8,128]{1,0:T(8,128)S(1)}, u32[]{:S(2)}, u32[]{:S(2)}) collective-permute-start(s32[8,128]{1,0:T(8,128)S(1)} %broadcast_in_dim.53), channel_id=1, source_target_pairs={{0,4},{4,0},{8,12},{12,8},{16,20},{20,16},{24,28},{28,24},{32,36},... | collective-permute-start | bytes 12296 | tf_op jit(solution)/shard_map/ppermute | solution.py:275
  15.8 18.8 %collective-permute-start.5 = (s32[8,128]{1,0:T(8,128)S(1)}, s32[8,128]{1,0:T(8,128)S(1)}, u32[]{:S(2)}, u32[]{:S(2)}) collective-permute-start(s32[8,128]{1,0:T(8,128)S(1)} %broadcast_select_fusion.4), channel_id=1, source_target_pairs={{0,16},{4,20},{8,24},{12,28},{16,32},{20,36},{24,40},{28,44},{32,4... | collective-permute-start | bytes 12296 | tf_op jit(solution)/shard_map/ppermute | solution.py:305
  20.4 11.2 %copy-start.6 = (s32[1,1,12,4]{2,3,1,0:T(4,128)S(1)}, s32[1,1,12,4]{2,3,1,0:T(4,128)}, u32[]{:S(2)}) copy-start(s32[1,1,12,4]{2,3,1,0:T(4,128)} %param.15) | copy-start | bytes 580
  20.5 23.5 %copy-start.7 = (s32[1,1,8]{2,1,0:T(1,128)S(1)}, s32[1,1,8]{2,1,0:T(1,128)}, u32[]{:S(2)}) copy-start(s32[1,1,8]{2,1,0:T(1,128)} %param.14) | copy-start | bytes 100
  20.5 12.7 %collective-permute-start.4 = (s32[8,128]{1,0:T(8,128)S(1)}, s32[8,128]{1,0:T(8,128)S(1)}, u32[]{:S(2)}, u32[]{:S(2)}) collective-permute-start(s32[8,128]{1,0:T(8,128)S(1)} %get-tuple-element.36), channel_id=1, source_target_pairs={{0,8},{4,12},{8,16},{12,20},{16,24},{20,28},{24,32},{28,36},{32,40... | collective-permute-start | bytes 12296 | tf_op jit(solution)/shard_map/ppermute | solution.py:304
  26.4 0.7 copy-start.4
  27.2 17.5 %collective-permute-start = (f32[512,128]{1,0:T(8,128)}, f32[512,128]{1,0:T(8,128)S(1)}, u32[]{:S(2)}, u32[]{:S(2)}) collective-permute-start(f32[512,128]{1,0:T(8,128)} %get-tuple-element.21), channel_id=1, source_target_pairs={{0,1},{1,2},{2,3},{3,0},{4,5},{5,6},{6,7},{7,4},{8,9},{9,10},{10,1... | collective-permute-start | bytes 786440 | tf_op jit(solution)/shard_map/ppermute | solution.py:247
  28.8 15.9 %collective-permute-start.1 = (f32[512,128]{1,0:T(8,128)}, f32[512,128]{1,0:T(8,128)S(1)}, u32[]{:S(2)}, u32[]{:S(2)}) collective-permute-start(f32[512,128]{1,0:T(8,128)} %get-tuple-element.22), channel_id=1, source_target_pairs={{0,2},{1,3},{2,0},{3,1},{4,6},{5,7},{6,4},{7,5},{8,10},{9,11},{10,... | collective-permute-start | bytes 786440 | tf_op jit(solution)/shard_map/ppermute | solution.py:247
  33.2 11.4 %collective-permute-start.2 = (f32[512,128]{1,0:T(8,128)}, f32[512,128]{1,0:T(8,128)S(1)}, u32[]{:S(2)}, u32[]{:S(2)}) collective-permute-start(f32[512,128]{1,0:T(8,128)} %copy-done.4), channel_id=1, source_target_pairs={{0,3},{1,0},{2,1},{3,2},{4,7},{5,4},{6,5},{7,6},{8,11},{9,8},{10,9... | collective-permute-start | bytes 786440 | tf_op jit(solution)/shard_map/ppermute | solution.py:247
  35.9 25.6 %collective-permute-start.11 = (f32[256,512]{1,0:T(8,128)S(1)}, f32[256,512]{1,0:T(8,128)S(1)}, u32[]{:S(2)}, u32[]{:S(2)}) collective-permute-start(f32[256,512]{1,0:T(8,128)S(1)} %get-tuple-element.39), channel_id=1, source_target_pairs={{0,8},{4,12},{8,16},{12,20},{16,24},{20,28},{24,32},{28,36},{32,40... | collective-permute-start | bytes 1572872 | tf_op jit(solution)/shard_map/ppermute | solution.py:294
  39.9 31.5 %collective-permute-start.12 = (f32[256,512]{1,0:T(8,128)S(1)}, f32[256,512]{1,0:T(8,128)S(1)}, u32[]{:S(2)}, u32[]{:S(2)}) collective-permute-start(f32[256,512]{1,0:T(8,128)S(1)} %get-tuple-element.38), channel_id=1, source_target_pairs={{0,16},{4,20},{8,24},{12,28},{16,32},{20,36},{24,40},{28,44},{32,4... | collective-permute-start | bytes 1572872 | tf_op jit(solution)/shard_map/ppermute | solution.py:295
  45.7 43.7 %copy-start.2 = (f32[512,128]{1,0:T(8,128)}, f32[512,128]{1,0:T(8,128)S(1)}, u32[]{:S(2)}) copy-start(f32[512,128]{1,0:T(8,128)S(1)} %bitcast_add_fusion.1.own) | copy-start | bytes 786436
  45.7 25.9 %collective-permute-start.6 = (f32[512,128]{1,0:T(8,128)S(1)}, f32[512,128]{1,0:T(8,128)S(1)}, u32[]{:S(2)}, u32[]{:S(2)}) collective-permute-start(f32[512,128]{1,0:T(8,128)S(1)} %bitcast_add_fusion.1.own), channel_id=1, source_target_pairs={{0,4},{4,0},{8,12},{12,8},{16,20},{20,16},{24,28},{28,24},{32,36},... | collective-permute-start | bytes 786440 | tf_op jit(solution)/shard_map/ppermute | solution.py:289
  71.5 12.4 %collective-permute-start.13 = (f32[256,512]{1,0:T(8,128)S(1)}, f32[256,512]{1,0:T(8,128)S(1)}, u32[]{:S(2)}, u32[]{:S(2)}) collective-permute-start(f32[256,512]{1,0:T(8,128)S(1)} %broadcast_select_fusion), channel_id=1, source_target_pairs={{0,4},{4,0},{8,12},{12,8},{16,20},{20,16},{24,28},{28,24},{32,36},... | collective-permute-start | bytes 1572872 | tf_op jit(solution)/shard_map/ppermute | solution.py:300
  71.6 10.4 %collective-permute-start.7 = (f32[256,128]{1,0:T(8,128)S(1)}, f32[256,128]{1,0:T(8,128)S(1)}, u32[]{:S(2)}, u32[]{:S(2)}) collective-permute-start(f32[256,128]{1,0:T(8,128)S(1)} %get-tuple-element.41), channel_id=1, source_target_pairs={{0,8},{4,12},{8,16},{12,20},{16,24},{20,28},{24,32},{28,36},{32,40... | collective-permute-start | bytes 393224 | tf_op jit(solution)/shard_map/ppermute | solution.py:294
  73.6 10.2 %collective-permute-start.8 = (f32[256,128]{1,0:T(8,128)S(1)}, f32[256,128]{1,0:T(8,128)S(1)}, u32[]{:S(2)}, u32[]{:S(2)}) collective-permute-start(f32[256,128]{1,0:T(8,128)S(1)} %get-tuple-element.40), channel_id=1, source_target_pairs={{0,16},{4,20},{8,24},{12,28},{16,32},{20,36},{24,40},{28,44},{32,4... | collective-permute-start | bytes 393224 | tf_op jit(solution)/shard_map/ppermute | solution.py:295
  81.0 1.0 copy-start.3
  83.8 5.6 %collective-permute-start.9 = (f32[256,128]{1,0:T(8,128)S(1)}, f32[256,128]{1,0:T(8,128)S(1)}, u32[]{:S(2)}, u32[]{:S(2)}) collective-permute-start(f32[256,128]{1,0:T(8,128)S(1)} %broadcast_select_fusion.1), channel_id=1, source_target_pairs={{0,4},{4,0},{8,12},{12,8},{16,20},{20,16},{24,28},{28,24},{32,36},... | collective-permute-start | bytes 393224 | tf_op jit(solution)/shard_map/ppermute | solution.py:300
  89.3 19.1 %copy-start.5 = (f32[1,1,512,128]{3,2,1,0:T(8,128)S(1)}, f32[1,1,512,128]{3,2,1,0:T(8,128)}, u32[]{:S(2)}) copy-start(f32[1,1,512,128]{3,2,1,0:T(8,128)} %param.17) | copy-start | bytes 786436
  92.2 15.6 %collective-permute-start.14 = (f32[512,128]{1,0:T(8,128)S(1)}, f32[512,128]{1,0:T(8,128)S(1)}, u32[]{:S(2)}, u32[]{:S(2)}) collective-permute-start(f32[512,128]{1,0:T(8,128)S(1)} %get-tuple-element.33), channel_id=1, source_target_pairs={{0,1},{1,2},{2,3},{3,0},{4,5},{5,6},{6,7},{7,4},{8,9},{9,10},{10,1... | collective-permute-start | bytes 786440 | tf_op jit(solution)/shard_map/ppermute | solution.py:247
  92.8 15.0 %collective-permute-start.15 = (f32[512,128]{1,0:T(8,128)S(1)}, f32[512,128]{1,0:T(8,128)S(1)}, u32[]{:S(2)}, u32[]{:S(2)}) collective-permute-start(f32[512,128]{1,0:T(8,128)S(1)} %get-tuple-element.34), channel_id=1, source_target_pairs={{0,2},{1,3},{2,0},{3,1},{4,6},{5,7},{6,4},{7,5},{8,10},{9,11},{10,... | collective-permute-start | bytes 786440 | tf_op jit(solution)/shard_map/ppermute | solution.py:247
  94.3 14.1 %collective-permute-start.16 = (f32[512,128]{1,0:T(8,128)S(1)}, f32[512,128]{1,0:T(8,128)S(1)}, u32[]{:S(2)}, u32[]{:S(2)}) collective-permute-start(f32[512,128]{1,0:T(8,128)S(1)} %get-tuple-element.35), channel_id=1, source_target_pairs={{0,3},{1,0},{2,1},{3,2},{4,7},{5,4},{6,5},{7,6},{8,11},{9,8},{10,9... | collective-permute-start | bytes 786440 | tf_op jit(solution)/shard_map/ppermute | solution.py:247

commit v2 on v0

v2 whole, which is shorter than its diff:
```python
import jax
import jax.numpy as jnp
from jax import lax
from jax.experimental import pallas as pl
from jax.experimental.pallas import tpu as pltpu
from jax.sharding import PartitionSpec as P

TB = 128
WT = 4
NA = 12
NB = 8
W = 512
SA = 1536
SB = 1536
OWN = 4
HALF = 256
SENT = HALF + 8
BLOCK = 2 * SENT
CHUNKS = 3
F32 = jnp.float32
BF16 = jnp.bfloat16
FIRST = ((0,), (0,))
PLAIN = ((1,), (0,))
ANY = pl.BlockSpec(memory_space=pl.ANY)


def split(x):
    high = x.astype(BF16)
    return high, (x - high.astype(F32)).astype(BF16)


def dot3(a, b, contract):
    def one(u, v):
        return lax.dot_general(u, v, (contract, ((), ())), preferred_element_type=F32)

    return one(a[0], b[0]) + (one(a[0], b[1]) + one(a[1], b[0]))


HELD = pl.BlockSpec(memory_space=pltpu.VMEM)


def whole(*shape):
    return pl.BlockSpec(shape, lambda *_: (0,) * len(shape))


def call(kernel, name, scalars, in_specs, operands, out_shapes, scratch=(), limit=24, out=HELD):
    many = isinstance(out_shapes, list)
    out_specs = [out] * len(out_shapes) if many else out
    return pl.pallas_call(
        kernel,
        grid_spec=pltpu.PrefetchScalarGridSpec(
            num_scalar_prefetch=len(scalars),
            grid=(1,),
            in_specs=in_specs,
            out_specs=out_specs,
            scratch_shapes=list(scratch),
        ),
        out_shape=out_shapes,
        compiler_params=pltpu.CompilerParams(vmem_limit_bytes=limit << 20),
        cost_estimate=pl.CostEstimate(flops=1 << 20, bytes_accessed=1 << 16, transcendentals=0),
        name=name,
    )(*scalars, *operands)


def f32(*shape):
    return jax.ShapeDtypeStruct(shape, F32)


def bf16(*shape):
    return jax.ShapeDtypeStruct(shape, BF16)


def place_among(tiles, count, tile):
    at, there = jnp.int32(0), jnp.int32(0)
    for j in range(count):
        same = (tiles(j) == tile).astype(jnp.int32)
        at, there = at + j * same, there + same
    return at, there


def store_slabs(full, place, slabs):
    for r in range(OWN):
        start = pl.multiple_of(lax.rem(place + r, OWN) * TB, TB)
        slabs[r][...] = full[:, pl.ds(start, TB)]


def halves(core):
    mine = pl.ds(pl.multiple_of(core * HALF, HALF), HALF)
    rest = pl.ds(pl.multiple_of((1 - core) * HALF, HALF), HALF)
    return mine, rest


def upper_rows_kernel(anc, parent, others_parent, where, top, u_ref, block, rows, factor, total, row_sems, u_sems):
    per = NA // CHUNKS
    size = per * TB

    def u_copy(c):
        part = pl.ds(c * size, size)
        return pltpu.make_async_copy(u_ref.at[0, part, :], factor.at[part, :], u_sems.at[c])

    def row_copy(j):
        start = pl.multiple_of(anc[0, j] * TB, TB)
        return pltpu.make_async_copy(top.at[pl.ds(start, TB), :], rows.at[pl.ds(j * TB, TB), :], row_sems.at[j])

    for c in range(CHUNKS):
        u_copy(c).start()
        for i in range(per):
            row_copy(c * per + i).start()
    for c in range(CHUNKS):
        u_copy(c).wait()
        for i in range(per):
            row_copy(c * per + i).wait()
        part = slice(c * size, (c + 1) * size)
        product = dot3(split(factor[part, :]), split(rows[part, :]), FIRST)
        if c == 0:
            total[...] = product
        else:
            total[...] += product
    for r in range(OWN):
        _, there = place_among(lambda j: anc[0, j], NA, where[0] * OWN + r)

        @pl.when(there == 0)
        def _():
            total[:, r * TB:(r + 1) * TB] = jnp.zeros((W, TB), F32)

    lane = lax.broadcasted_iota(jnp.int32, (SENT - HALF, W), 1)
    marks = jnp.where(lane == NA, parent[0], jnp.where(lane == NA + 1, others_parent[0], 0))
    for j in range(NA):
        marks = jnp.where(lane == j, anc[0, j], marks)
    for h in range(2):
        block[h * SENT:h * SENT + HALF, :] = total[h * HALF:(h + 1) * HALF, :]
        block[h * SENT + HALF:(h + 1) * SENT, :] = marks.astype(F32)


def upper_sum_kernel(anc, where, block, u_ref, s0, s1, s2, s3, tiles, full, sems):
    def copy(r, at):
        rows = pl.ds(pl.multiple_of(at * TB, TB), TB)
        return pltpu.make_async_copy(u_ref.at[0, rows, :], tiles.at[pl.ds(r * TB, TB), :], sems.at[r])

    found = [place_among(lambda j: anc[0, j], NA, where[0] * OWN + r) for r in range(OWN)]
    for r in range(OWN):
        copy(r, found[r][0]).start()
    for r in range(OWN):
        copy(r, found[r][0]).wait()
    own = split(
        jnp.concatenate(
            [jnp.where(found[r][1] > 0, tiles[r * TB:(r + 1) * TB, :], 0.0) for r in range(OWN)], axis=0
        )
    )
    for h in range(2):
        full[h * HALF:(h + 1) * HALF, :] = dot3(split(block[h * SENT:h * SENT + HALF, :]), own, PLAIN)
    store_slabs(full, where[0], (s0, s1, s2, s3))


def lower_prepare_kernel(pattern, u_ref, high, low):
    for i in range(WT + NB):
        for j in range(WT):
            rows, cols = slice(i * TB, (i + 1) * TB), slice(j * TB, (j + 1) * TB)
            masked = u_ref[0, 0, rows, cols] * pattern[i * WT + j].astype(F32)
            high[rows, cols], low[rows, cols] = split(masked)


def after_kernel(array, earlier, same):
    pass


def after(array, earlier):
    return pl.pallas_call(
        after_kernel,
        in_specs=[ANY, ANY],
        out_specs=ANY,
        out_shape=jax.ShapeDtypeStruct(array.shape, array.dtype),
        input_output_aliases={0: 0},
        cost_estimate=pl.CostEstimate(flops=1, bytes_accessed=1, transcendentals=0),
        name="after",
    )(array, earlier)


def take_marks_kernel(array, same, marks, sem):
    copy = pltpu.make_async_copy(array.at[pl.ds(HALF, SENT - HALF), :], marks, sem)
    copy.start()
    copy.wait()


def take_marks(array):
    return pl.pallas_call(
        take_marks_kernel,
        in_specs=[ANY],
        out_specs=[ANY, HELD],
        out_shape=[jax.ShapeDtypeStruct(array.shape, F32), f32(SENT - HALF, W)],
        scratch_shapes=[pltpu.SemaphoreType.DMA],
        input_output_aliases={0: 0},
        cost_estimate=pl.CostEstimate(flops=1, bytes_accessed=1, transcendentals=0),
        name="take_marks",
    )(array)


def fetch(choice, copies):
    for c, some in enumerate(copies):
        @pl.when(choice == c)
        def _():
            for copy in some:
                copy.start()
            for copy in some:
                copy.wait()


def lower_cross_kernel(code, where, far_tiles, own, other, near, swapped, far, *refs):
    high, low, p_ref, block, value, sems = refs[NB:]
    mine, rest = halves(where[1])
    part = pl.ds(0, HALF)
    second = pl.ds(SENT, HALF)

    def full(ref):
        return [
            pltpu.make_async_copy(ref.at[part, :], block.at[pl.ds(0, HALF), :], sems.at[0]),
            pltpu.make_async_copy(ref.at[second, :], block.at[pl.ds(HALF, HALF), :], sems.at[1]),
        ]

    fetch(
        code[0],
        [
            full(own),
            full(other),
            [
                pltpu.make_async_copy(near.at[part, :], block.at[mine, :], sems.at[0]),
                pltpu.make_async_copy(swapped.at[part, :], block.at[rest, :], sems.at[1]),
            ],
            full(far),
        ],
    )
    rows = split(jnp.concatenate([g[...] for g in refs[:NB]], axis=0) * 0.5)
    value[...] = dot3((high[W:, :], low[W:, :]), rows, FIRST) - dot3((high[:W, :], low[:W, :]), split(block[...]), FIRST)
    own_high, own_low = [], []
    for r in range(OWN):
        at, there = place_among(lambda j: far_tiles[j], NB, where[0] * OWN + r)

        @pl.when(there == 0)
        def _():
            value[:, r * TB:(r + 1) * TB] = jnp.zeros((W, TB), F32)

        rows = pl.ds(pl.multiple_of(W + at * TB, TB), TB)
        own_high.append(high[rows, :])
        own_low.append(low[rows, :])
    rows_of_own = jnp.concatenate(own_high, axis=0), jnp.concatenate(own_low, axis=0)
    product = dot3(split(value[...]), rows_of_own, PLAIN)
    p_ref[...] = product + product.T


def lower_sum_kernel(code, where, own, even, near, swapped, far, p_ref, high, low, s0, s1, s2, s3, block, full, sem):
    fetch(code[1], [[pltpu.make_async_copy(ref, block, sem)] for ref in (own, even, near, swapped, far)])
    inner = dot3(split(block[...]), (high[:W, :], low[:W, :]), FIRST)
    rows = pl.ds(pl.multiple_of(where[0] * TB, TB), TB)
    full[...] = p_ref[...] + dot3(split(inner), (high[rows, :], low[rows, :]), FIRST)
    store_slabs(full, where[0], (s0, s1, s2, s3))


def to_owners(slabs, count):
    ways = [[(i, (i + r) % count) for i in range(count)] for r in range(count)]
    arrived = [lax.ppermute(slabs[r], "tile", ways[r]) for r in (2, 1, 3)]
    return slabs[0], arrived[1], arrived[0], arrived[2]


def body(top, anc_a, u_a, dinv_a, parent, sel_b, pattern, u_b, dinv_b):
    leaves = lax.axis_size("leaf")
    count = lax.axis_size("tile")
    place = lax.axis_index("tile").astype(jnp.int32)
    leaf = lax.axis_index("leaf").astype(jnp.int32)
    core = leaf % 2
    even = core == 0
    where = jnp.stack([place, core, leaf])
    swap = [(i, i ^ 1) for i in range(leaves)]
    next_chip = [(i, i + 2) for i in range(leaves - 2)]
    crossing = [(i, (i + 2) ^ 1) for i in range(leaves - 2)]
    odd_on = [(i, i + 3) for i in range(1, leaves - 3, 2)]

    others_parent = lax.ppermute(parent, "leaf", swap)
    block = call(
        upper_rows_kernel, "upper_rows", (anc_a, parent, others_parent, where), [ANY, ANY], (top, u_a), f32(BLOCK, W),
        [pltpu.VMEM((SA, W), F32), pltpu.VMEM((SA, W), F32), pltpu.VMEM((W, W), F32),
         pltpu.SemaphoreType.DMA((NA,)), pltpu.SemaphoreType.DMA((CHUNKS,))],
    )
    slabs_a = call(
        upper_sum_kernel, "upper_sum", (anc_a, where), [HELD, ANY], (block, u_a), [f32(W, TB)] * 4,
        [pltpu.VMEM((W, W), F32), pltpu.VMEM((W, W), F32), pltpu.SemaphoreType.DMA((OWN,))],
    )
    other = lax.ppermute(block, "leaf", swap)
    odd_heads = jnp.where(even, others_parent[0], parent[0]) == leaf - core + 1
    latest = jnp.where(
        jnp.logical_xor(even, odd_heads),
        lax.dynamic_slice_in_dim(block, core * SENT, SENT, 0),
        lax.dynamic_slice_in_dim(other, core * SENT, SENT, 0),
    )
    near = lax.ppermute(latest, "leaf", next_chip)
    far = lax.ppermute(block, "leaf", odd_on)

    high, low = call(
        lower_prepare_kernel, "lower_prepare", (pattern.reshape(-1),), [whole(1, 1, SB, W)], (u_b,), [bf16(SB, W)] * 2,
    )
    own, next_one, opposite, last_one = to_owners(slabs_a, count)
    sigma_a = dinv_a[0] + ((own + next_one) + (opposite + last_one))
    near_s = lax.ppermute(sigma_a, "leaf", crossing)
    far_s = lax.ppermute(sigma_a, "leaf", odd_on)

    head = parent[0]
    back = leaf - head
    from_far = jnp.logical_and(even, back == 3)
    from_even = jnp.logical_and(jnp.logical_not(even), back == 1)
    code_x = jnp.where(back == 0, 0, jnp.where(from_even, 1, jnp.where(from_far, 3, 2)))
    direct = jnp.where(head % 2 == 1 - core, 2, 3)
    code_s = jnp.where(back == 0, 0, jnp.where(from_even, 1, jnp.where(from_far, 4, direct)))
    code = jnp.stack([code_x, code_s]).astype(jnp.int32)

    near, near_marks = take_marks(after(near, sigma_a))
    swapped = lax.ppermute(near, "leaf", swap)
    marked = jnp.where(
        code_x == 0, block[HALF:SENT], jnp.where(code_x == 1, other[HALF:SENT], jnp.where(code_x == 3, far[HALF:SENT], near_marks))
    )[0, :NA].astype(jnp.int32)
    far_tiles = jnp.sum(
        jnp.where(sel_b[0, 0][:, None] == jnp.arange(NA, dtype=jnp.int32)[None], marked[None], 0), axis=1
    )
    p = call(
        lower_cross_kernel, "lower_cross", (code, where, far_tiles),
        [ANY] * 5 + [pl.BlockSpec((TB, W), lambda k, code, where, tiles, j=j: (tiles[j], 0)) for j in range(NB)] + [HELD] * 2,
        (block, other, near, swapped, far) + (top,) * NB + (high, low),
        f32(W, W), [pltpu.VMEM((W, W), F32), pltpu.VMEM((W, W), F32), pltpu.SemaphoreType.DMA((2,))],
    )
    near_s = after(near_s, far_s)
    swapped_s = lax.ppermute(near_s, "leaf", swap)
    other_s = lax.ppermute(sigma_a, "leaf", swap)
    slabs_b = call(
        lower_sum_kernel, "lower_sum", (code, where), [ANY] * 5 + [HELD] * 3,
        (sigma_a, other_s, near_s, swapped_s, far_s, p, high, low), [f32(W, TB)] * 4,
        [pltpu.VMEM((W, TB), F32), pltpu.VMEM((W, W), F32), pltpu.SemaphoreType.DMA],
    )
    own, next_one, opposite, last_one = to_owners(slabs_b, count)
    sigma_b = dinv_b + ((own + next_one) + (opposite + last_one))[None, None]
    return sigma_a[None], sigma_b


def solution(mesh):
    in_specs = (
        P(None, "tile"),
        P("leaf", None),
        P("leaf", None, None),
        P("leaf", None, "tile"),
        P("leaf"),
        P("leaf", None, None),
        P("leaf", None, None, None),
        P("leaf", None, None, None),
        P("leaf", None, None, "tile"),
    )
    out_specs = (P("leaf", None, "tile"), P("leaf", None, None, "tile"))
    return jax.shard_map(body, mesh=mesh, in_specs=in_specs, out_specs=out_specs, check_vma=False)
```

time: 749 us -> 87.1 us (0.12); the launches traced: 734 us -> 86 us
  waiting for transfers between devices: 332 us -> 22.3 us
  other arithmetic: 238 us -> 2.64 us
  blocking collectives: 56 us -> 0 us
  matrix products: 46.8 us -> 0 us
  local copies, waits for them, and re-layouts: 44.5 us -> 17.9 us
  starting transfers between devices: 0.34 us -> 24.2 us
  Pallas kernels: 0 us -> 16.8 us
  between operations: 14.8 us -> 2.12 us
    select_n x110 -> x1, other arithmetic: 200 us -> 0.08 us  [body(): jnp.where(jnp.logical_xor(even, odd_heads), lax.dynamic_slice_in_dim(bloc...]
    all_gather x1 -> x0, waiting for transfers between devices: 160 us -> none  [entering(): gathered = jax.tree.map(lambda a: lax.all_gather(a, axis), part)]
    psum x1 -> x0, waiting for transfers between devices: 103 us -> none  [body(): far_full = lax.psum(far_partial, 'tile')]
    reduce_scatter x2 -> x0, waiting for transfers between devices: 67.9 us -> none  [the longest x1 39.3 us: body(): lax.psum_scatter(lax.dot_general(slice_part, rows_upper, (((0,), (1,)), (...]
    dot_general x9 -> x0, matrix products: 46.8 us -> none  [the longest x1 12.2 us: body(): lax.dot_general(slice_part, rows_upper, (((0,), (1,)), ((), ())), precisi...]
    all_gather x1 -> x0, blocking collectives: 38.9 us -> none  [entering(): gathered = jax.tree.map(lambda a: lax.all_gather(a, axis), part)]
    gt x50 -> x0, other arithmetic: 30.8 us -> none  [take_latter(): take_new = latter[0] > 0]
    ppermute x0 -> x15, starting transfers between devices: none -> 24.2 us  [the longest x6 9.83 us: to_owners(): arrived = [lax.ppermute(slabs[r], 'tile', ways[r]) for r in (2, 1, 3)]]
  transfers between devices with their start and end apart: 4 -> 15, of which waited for: 4 -> 7; matrix products, arithmetic and copies ran while one was open for 4% -> 3% of each run, Pallas kernels for 0% -> 11%
where the time goes in v2:
time: 87.1 us; the launch traced here: 86 us
  starting transfers between devices  24.2 us (28%)
  waiting for transfers between devices  22.3 us (26%)
  local copies, waits for them, and re-layouts  17.9 us (21%)
  Pallas kernels  16.8 us (19%)
  other arithmetic  2.64 us (3%)
  between operations  2.12 us (2%)
    unnamed x41, local copies, waits for them, and re-layouts  17.1 us
    ppermute x6, waiting for transfers between devices, to_owners(): arrived = [lax.ppermute(slabs[r], 'tile', ways[r]) for r in (2, 1, 3)]  16.8 us
    pallas_call x5, Pallas kernels, call(): pl.pallas_call(kernel, grid_spec=pltpu.PrefetchScalarGridSpec(num_scalar_...  15.5 us
    ppermute x6, starting transfers between devices, to_owners(): arrived = [lax.ppermute(slabs[r], 'tile', ways[r]) for r in (2, 1, 3)]  9.83 us
    ppermute x1, starting transfers between devices, body(): near_s = lax.ppermute(sigma_a, 'leaf', crossing)  5.23 us
    ppermute x1, waiting for transfers between devices, body(): far_s = lax.ppermute(sigma_a, 'leaf', odd_on)  4.79 us
    ppermute x1, starting transfers between devices, body(): near = lax.ppermute(latest, 'leaf', next_chip)  3.38 us
    ppermute x1, starting transfers between devices, body(): swapped = lax.ppermute(near, 'leaf', swap)  2.74 us
  transfers between devices with their start and end apart: 15, of which 7 were waited for; matrix products, arithmetic and copies ran while one was open for 3% of the time, Pallas kernels for 11%

profile of v2, /device:TPU:194, one launch (start us, length us, event | category | flops | bytes accessed | tf_op | source)
XLA Modules:
  0.0 86.0 jit_solution(807398713341807136)
XLA Ops:
  2.1 2.2 %copy-done = f32[2048,512]{1,0:T(8,128)S(1)} copy-done((f32[2048,512]{1,0:T(8,128)S(1)}, f32[2048,512]{1,0:T(8,128)}, u32[]{:S(2)}) %copy-start) | copy-done | bytes 4194328
  4.3 1.9 %copy-done.2 = f32[1,1536,512]{2,1,0:T(8,128)S(1)} copy-done((f32[1,1536,512]{2,1,0:T(8,128)S(1)}, f32[1,1536,512]{2,1,0:T(8,128)}, u32[]{:S(2)}) %copy-start.2) | copy-done | bytes 3145752
  6.8 4.8 %upper_rows.1.block.own = f32[528,512]{1,0:T(8,128)S(1)} custom-call(s32[1,12]{1,0:T(1,128)S(1)} %copy-done.14, s32[1]{0:T(128)} %copy.20.parent, s32[1]{0:T(128)} %collective-permute-done.others_parent, s32[3]{0:T(128)S(1)} %pad_add_fusion.where, f32[2048,512]{1,0:T(8,128)S(1)} %copy-done, f32[1,1536,512]{2,1,0:T(8,128)S(1)} %copy-done.2), custom_call_target="tpu_custom_call" | custom-call | flops 1048576 | bytes 65536 | tf_op jit(solution)/shard_map/upper_rows/pallas_call | solution.py:49
  11.9 1.3 %collective-permute-start.9 = (f32[528,512]{1,0:T(8,128)S(1)}, f32[528,512]{1,0:T(8,128)}, u32[]{:S(2)}, u32[]{:S(2)}) collective-permute-start(f32[528,512]{1,0:T(8,128)S(1)} %upper_rows.1.block.own), channel_id=1, source_target_pairs={{4,16},{12,24},{20,32},{28,40},{36,48},{44,56},{52,64},{60,72},{68... | collective-permute-start | bytes 3244040 | tf_op jit(solution)/shard_map/ppermute | solution.py:295
  13.8 1.9 %copy-done.3 = f32[1,1536,512]{2,1,0:T(8,128)S(1)} copy-done((f32[1,1536,512]{2,1,0:T(8,128)S(1)}, f32[1,1536,512]{2,1,0:T(8,128)}, u32[]{:S(2)}) %copy-start.3) | copy-done | bytes 3145752
  15.7 2.0 %upper_sum.1 = (f32[512,128]{1,0:T(8,128)S(1)}, f32[512,128]{1,0:T(8,128)S(1)}, f32[512,128]{1,0:T(8,128)S(1)}, f32[512,128]{1,0:T(8,128)S(1)}) custom-call(s32[1,12]{1,0:T(1,128)S(1)} %copy-done.15, s32[3]{0:T(128)S(1)} %pad_add_fusion.where, f32[528,512]{1,0:T(8,128)S(1)} %upper_rows.1.block.own, f32[1,1536,512]{2,1,0:T(8,128)S(1)} %copy-done.3), custom_call_target="tpu_custom_call" | custom-call | flops 1048576 | bytes 65536 | tf_op jit(solution)/shard_map/upper_sum/pallas_call | solution.py:49
  17.7 1.7 %collective-permute-start.1 = (f32[512,128]{1,0:T(8,128)S(1)}, f32[512,128]{1,0:T(8,128)S(1)}, u32[]{:S(2)}, u32[]{:S(2)}) collective-permute-start(f32[512,128]{1,0:T(8,128)S(1)} %get-tuple-element.15), channel_id=1, source_target_pairs={{0,1},{1,2},{2,3},{3,0},{4,5},{5,6},{6,7},{7,4},{8,9},{9,10},{10,1... | collective-permute-start | bytes 786440 | tf_op jit(solution)/shard_map/ppermute | solution.py:260
  19.4 2.9 %collective-permute-start.2 = (f32[512,128]{1,0:T(8,128)S(1)}, f32[512,128]{1,0:T(8,128)S(1)}, u32[]{:S(2)}, u32[]{:S(2)}) collective-permute-start(f32[512,128]{1,0:T(8,128)S(1)} %get-tuple-element.16), channel_id=1, source_target_pairs={{0,2},{1,3},{2,0},{3,1},{4,6},{5,7},{6,4},{7,5},{8,10},{9,11},{10,... | collective-permute-start | bytes 786440 | tf_op jit(solution)/shard_map/ppermute | solution.py:260
  22.3 1.3 %collective-permute-start.3 = (f32[512,128]{1,0:T(8,128)S(1)}, f32[512,128]{1,0:T(8,128)S(1)}, u32[]{:S(2)}, u32[]{:S(2)}) collective-permute-start(f32[512,128]{1,0:T(8,128)S(1)} %get-tuple-element.17), channel_id=1, source_target_pairs={{0,3},{1,0},{2,1},{3,2},{4,7},{5,4},{6,5},{7,6},{8,11},{9,8},{10,9... | collective-permute-start | bytes 786440 | tf_op jit(solution)/shard_map/ppermute | solution.py:260
  23.6 1.0 %copy-done.10 = f32[528,512]{1,0:T(8,128)} copy-done((f32[528,512]{1,0:T(8,128)}, f32[528,512]{1,0:T(8,128)S(1)}, u32[]{:S(2)}) %copy-start.10) | copy-done | bytes 1081368
  24.7 3.4 %collective-permute-start.10 = (f32[264,512]{1,0:T(8,128)S(1)}, f32[264,512]{1,0:T(8,128)S(1)}, u32[]{:S(2)}, u32[]{:S(2)}) collective-permute-start(f32[264,512]{1,0:T(8,128)S(1)} %dynamic-slice_select_fusion), channel_id=1, source_target_pairs={{0,8},{4,12},{8,16},{12,20},{16,24},{20,28},{24,32},{28,36},{32,40... | collective-permute-start | bytes 1622024 | tf_op jit(solution)/shard_map/ppermute | solution.py:294
  28.1 4.0 %collective-permute-done.2 = f32[512,128]{1,0:T(8,128)S(1)} collective-permute-done((f32[512,128]{1,0:T(8,128)S(1)}, f32[512,128]{1,0:T(8,128)S(1)}, u32[]{:S(2)}, u32[]{:S(2)}) %collective-permute-start.2) | collective-permute-done | bytes 262176 | tf_op jit(solution)/shard_map/ppermute | solution.py:260
  32.6 0.8 bitcast_add_fusion.1.earlier.own
  33.4 5.2 %collective-permute-start.5 = (f32[512,128]{1,0:T(8,128)}, f32[512,128]{1,0:T(8,128)}, u32[]{:S(2)}, u32[]{:S(2)}) collective-permute-start(f32[512,128]{1,0:T(8,128)} %bitcast_add_fusion.1.earlier.own), channel_id=1, source_target_pairs={{0,12},{4,8},{8,20},{12,16},{16,28},{20,24},{24,36},{28,32},{32,44... | collective-permute-start | bytes 786440 | tf_op jit(solution)/shard_map/ppermute | solution.py:302
  38.7 1.3 %collective-permute-start.6 = (f32[512,128]{1,0:T(8,128)}, f32[512,128]{1,0:T(8,128)S(1)}, u32[]{:S(2)}, u32[]{:S(2)}) collective-permute-start(f32[512,128]{1,0:T(8,128)} %bitcast_add_fusion.1.earlier.own), channel_id=1, source_target_pairs={{4,16},{12,24},{20,32},{28,40},{36,48},{44,56},{52,64},{60,72},{68... | collective-permute-start | bytes 786440 | tf_op jit(solution)/shard_map/ppermute | solution.py:303
  40.0 0.8 copy-done.7
  40.8 1.3 %take_marks.1 = (f32[264,512]{1,0:T(8,128)}, f32[8,512]{1,0:T(8,128)}) custom-call(f32[264,512]{1,0:T(8,128)} %after.3.array), custom_call_target="tpu_custom_call", output_to_operand_aliasing={{0}: (0, {})} | custom-call | flops 1 | bytes 1 | tf_op jit(solution)/shard_map/take_marks/pallas_call | solution.py:186
  42.1 2.7 %collective-permute-start.11 = (f32[264,512]{1,0:T(8,128)}, f32[264,512]{1,0:T(8,128)}, u32[]{:S(2)}, u32[]{:S(2)}) collective-permute-start(f32[264,512]{1,0:T(8,128)} %get-tuple-element.19.near), channel_id=1, source_target_pairs={{0,4},{4,0},{8,12},{12,8},{16,20},{20,16},{24,28},{28,24},{32,36},... | collective-permute-start | bytes 1622024 | tf_op jit(solution)/shard_map/ppermute | solution.py:315
  45.0 1.9 %copy-done.9 = f32[1,1,1536,512]{3,2,1,0:T(8,128)S(1)} copy-done((f32[1,1,1536,512]{3,2,1,0:T(8,128)S(1)}, f32[1,1,1536,512]{3,2,1,0:T(8,128)}, u32[]{:S(2)}) %copy-start.9) | copy-done | bytes 3145752
  46.9 1.2 %lower_prepare.1 = (bf16[1536,512]{1,0:T(8,128)(2,1)S(1)}, bf16[1536,512]{1,0:T(8,128)(2,1)S(1)}) custom-call(s32[48]{0:T(128)S(1)} %reshape.8.pattern, f32[1,1,1536,512]{3,2,1,0:T(8,128)S(1)} %copy-done.9), custom_call_target="tpu_custom_call" | custom-call | flops 1048576 | bytes 65536 | tf_op jit(solution)/shard_map/lower_prepare/pallas_call | solution.py:49
  48.1 1.2 %copy-done.4 = bf16[1536,512]{1,0:T(8,128)(2,1)} copy-done((bf16[1536,512]{1,0:T(8,128)(2,1)}, bf16[1536,512]{1,0:T(8,128)(2,1)S(1)}, u32[]{:S(2)}) %copy-start.4) | copy-done | bytes 1572888
  49.5 4.8 %collective-permute-done.6.earlier.far = f32[512,128]{1,0:T(8,128)S(1)} collective-permute-done((f32[512,128]{1,0:T(8,128)}, f32[512,128]{1,0:T(8,128)S(1)}, u32[]{:S(2)}, u32[]{:S(2)}) %collective-permute-start.6) | collective-permute-done | bytes 262176 | tf_op jit(solution)/shard_map/ppermute | solution.py:303
  55.0 0.7 slice.18
  56.6 2.2 %copy-done.1 = f32[2048,512]{1,0:T(8,128)S(1)} copy-done((f32[2048,512]{1,0:T(8,128)S(1)}, f32[2048,512]{1,0:T(8,128)}, u32[]{:S(2)}) %copy-start.1) | copy-done | bytes 4194328
  58.8 1.4 %copy-done.5 = bf16[1536,512]{1,0:T(8,128)(2,1)S(1)} copy-done((bf16[1536,512]{1,0:T(8,128)(2,1)S(1)}, bf16[1536,512]{1,0:T(8,128)(2,1)}, u32[]{:S(2)}) %copy-start.5) | copy-done | bytes 1572888
  60.2 1.2 %copy-done.11 = f32[528,512]{1,0:T(8,128)S(1)} copy-done((f32[528,512]{1,0:T(8,128)S(1)}, f32[528,512]{1,0:T(8,128)}, u32[]{:S(2)}) %copy-start.11) | copy-done | bytes 1081368
  61.4 4.9 %lower_cross.1.p_ref = f32[512,512]{1,0:T(8,128)S(1)} custom-call(s32[2]{0:T(128)S(1)} %pad_add_fusion.1.code, s32[3]{0:T(128)S(1)} %pad_add_fusion.where, s32[8]{0:T(128)S(1)} %select_reduce_fusion.far_tiles, f32[528,512]{1,0:T(8,128)S(1)} %upper_rows.1.block.own, f32[528,512]{1,0:T(8,128)S(1)} %copy-done.11, f32[264,512]{1,0:T(8,128)S(1)} %copy-done.8, ...), custom_call_target="tpu_custom_call" | custom-call | flops 1048576 | bytes 65536 | tf_op jit(solution)/shard_map/lower_cross/pallas_call | solution.py:49
  66.4 2.6 %lower_sum.1 = (f32[512,128]{1,0:T(8,128)S(1)}, f32[512,128]{1,0:T(8,128)S(1)}, f32[512,128]{1,0:T(8,128)S(1)}, f32[512,128]{1,0:T(8,128)S(1)}) custom-call(s32[2]{0:T(128)S(1)} %pad_add_fusion.1.code, s32[3]{0:T(128)S(1)} %pad_add_fusion.where, f32[512,128]{1,0:T(8,128)} %bitcast_add_fusion.1.earlier.own, f32[512,128]{1,0:T(8,128)} %collective-permute-done.4.even, ...), custom_call_target="tpu_custom_call" | custom-call | flops 1048576 | bytes 65536 | tf_op jit(solution)/shard_map/lower_sum/pallas_call | solution.py:49
  69.1 3.5 %collective-permute-start.13 = (f32[512,128]{1,0:T(8,128)S(1)}, f32[512,128]{1,0:T(8,128)S(1)}, u32[]{:S(2)}, u32[]{:S(2)}) collective-permute-start(f32[512,128]{1,0:T(8,128)S(1)} %get-tuple-element.24), channel_id=1, source_target_pairs={{0,2},{1,3},{2,0},{3,1},{4,6},{5,7},{6,4},{7,5},{8,10},{9,11},{10,... | collective-permute-start | bytes 786440 | tf_op jit(solution)/shard_map/ppermute | solution.py:260
  72.9 6.1 %collective-permute-done.12 = f32[512,128]{1,0:T(8,128)S(1)} collective-permute-done((f32[512,128]{1,0:T(8,128)S(1)}, f32[512,128]{1,0:T(8,128)S(1)}, u32[]{:S(2)}, u32[]{:S(2)}) %collective-permute-start.12) | collective-permute-done | bytes 262176 | tf_op jit(solution)/shard_map/ppermute | solution.py:260
  79.1 5.9 %collective-permute-done.13 = f32[512,128]{1,0:T(8,128)S(1)} collective-permute-done((f32[512,128]{1,0:T(8,128)S(1)}, f32[512,128]{1,0:T(8,128)S(1)}, u32[]{:S(2)}, u32[]{:S(2)}) %collective-permute-start.13) | collective-permute-done | bytes 262176 | tf_op jit(solution)/shard_map/ppermute | solution.py:260
  85.2 0.8 bitcast_add_fusion
  (59 shorter events, 5.1 us)
Async XLA Ops:
  0.6 1.5 %collective-permute-start = (s32[1]{0:T(128)}, s32[1]{0:T(128)}, u32[]{:S(2)}, u32[]{:S(2)}) collective-permute-start(s32[1]{0:T(128)} %param.13), channel_id=1, source_target_pairs={{0,4},{4,0},{8,12},{12,8},{16,20},{20,16},{24,28},{28,24},{32,36},... | collective-permute-start | bytes 20 | tf_op jit(solution)/shard_map/ppermute | solution.py:277
  2.1 2.2 %copy-start = (f32[2048,512]{1,0:T(8,128)S(1)}, f32[2048,512]{1,0:T(8,128)}, u32[]{:S(2)}) copy-start(f32[2048,512]{1,0:T(8,128)} %refs_7_.1) | copy-start | bytes 12582916
  4.3 1.9 %copy-start.2 = (f32[1,1536,512]{2,1,0:T(8,128)S(1)}, f32[1,1536,512]{2,1,0:T(8,128)}, u32[]{:S(2)}) copy-start(f32[1,1536,512]{2,1,0:T(8,128)} %u_ref.4) | copy-start | bytes 9437188
  6.8 7.0 %copy-start.15 = (s32[1,12]{1,0:T(1,128)S(1)}, s32[1,12]{1,0:T(1,128)}, u32[]{:S(2)}) copy-start(s32[1,12]{1,0:T(1,128)} %anc.3) | copy-start | bytes 148
  11.7 12.0 %collective-permute-start.8 = (f32[528,512]{1,0:T(8,128)S(1)}, f32[528,512]{1,0:T(8,128)S(1)}, u32[]{:S(2)}, u32[]{:S(2)}) collective-permute-start(f32[528,512]{1,0:T(8,128)S(1)} %upper_rows.1.block.own), channel_id=1, source_target_pairs={{0,4},{4,0},{8,12},{12,8},{16,20},{20,16},{24,28},{28,24},{32,36},... | collective-permute-start | bytes 3244040 | tf_op jit(solution)/shard_map/ppermute | solution.py:287
  11.9 43.1 %collective-permute-start.9 = (f32[528,512]{1,0:T(8,128)S(1)}, f32[528,512]{1,0:T(8,128)}, u32[]{:S(2)}, u32[]{:S(2)}) collective-permute-start(f32[528,512]{1,0:T(8,128)S(1)} %upper_rows.1.block.own), channel_id=1, source_target_pairs={{4,16},{12,24},{20,32},{28,40},{36,48},{44,56},{52,64},{60,72},{68... | collective-permute-start | bytes 3244040 | tf_op jit(solution)/shard_map/ppermute | solution.py:295
  13.8 1.9 %copy-start.3 = (f32[1,1536,512]{2,1,0:T(8,128)S(1)}, f32[1,1536,512]{2,1,0:T(8,128)}, u32[]{:S(2)}) copy-start(f32[1,1536,512]{2,1,0:T(8,128)} %u_ref.4) | copy-start | bytes 9437188
  17.7 14.9 %copy-start.16 = (f32[1,512,128]{2,1,0:T(8,128)S(1)}, f32[1,512,128]{2,1,0:T(8,128)}, u32[]{:S(2)}) copy-start(f32[1,512,128]{2,1,0:T(8,128)} %param.12) | copy-start | bytes 786436
  17.7 10.4 %collective-permute-start.1 = (f32[512,128]{1,0:T(8,128)S(1)}, f32[512,128]{1,0:T(8,128)S(1)}, u32[]{:S(2)}, u32[]{:S(2)}) collective-permute-start(f32[512,128]{1,0:T(8,128)S(1)} %get-tuple-element.15), channel_id=1, source_target_pairs={{0,1},{1,2},{2,3},{3,0},{4,5},{5,6},{6,7},{7,4},{8,9},{9,10},{10,1... | collective-permute-start | bytes 786440 | tf_op jit(solution)/shard_map/ppermute | solution.py:260
  19.4 12.7 %collective-permute-start.2 = (f32[512,128]{1,0:T(8,128)S(1)}, f32[512,128]{1,0:T(8,128)S(1)}, u32[]{:S(2)}, u32[]{:S(2)}) collective-permute-start(f32[512,128]{1,0:T(8,128)S(1)} %get-tuple-element.16), channel_id=1, source_target_pairs={{0,2},{1,3},{2,0},{3,1},{4,6},{5,7},{6,4},{7,5},{8,10},{9,11},{10,... | collective-permute-start | bytes 786440 | tf_op jit(solution)/shard_map/ppermute | solution.py:260
  22.3 10.3 %collective-permute-start.3 = (f32[512,128]{1,0:T(8,128)S(1)}, f32[512,128]{1,0:T(8,128)S(1)}, u32[]{:S(2)}, u32[]{:S(2)}) collective-permute-start(f32[512,128]{1,0:T(8,128)S(1)} %get-tuple-element.17), channel_id=1, source_target_pairs={{0,3},{1,0},{2,1},{3,2},{4,7},{5,4},{6,5},{7,6},{8,11},{9,8},{10,9... | collective-permute-start | bytes 786440 | tf_op jit(solution)/shard_map/ppermute | solution.py:260
  24.7 15.2 %collective-permute-start.10 = (f32[264,512]{1,0:T(8,128)S(1)}, f32[264,512]{1,0:T(8,128)S(1)}, u32[]{:S(2)}, u32[]{:S(2)}) collective-permute-start(f32[264,512]{1,0:T(8,128)S(1)} %dynamic-slice_select_fusion), channel_id=1, source_target_pairs={{0,8},{4,12},{8,16},{12,20},{16,24},{20,28},{24,32},{28,36},{32,40... | collective-permute-start | bytes 1622024 | tf_op jit(solution)/shard_map/ppermute | solution.py:294
  32.6 12.2 %copy-start.18 = (s32[1,1,12,4]{2,3,1,0:T(4,128)S(1)}, s32[1,1,12,4]{2,3,1,0:T(4,128)}, u32[]{:S(2)}) copy-start(s32[1,1,12,4]{2,3,1,0:T(4,128)} %param.15) | copy-start | bytes 580
  33.4 16.1 %collective-permute-start.5 = (f32[512,128]{1,0:T(8,128)}, f32[512,128]{1,0:T(8,128)}, u32[]{:S(2)}, u32[]{:S(2)}) collective-permute-start(f32[512,128]{1,0:T(8,128)} %bitcast_add_fusion.1.earlier.own), channel_id=1, source_target_pairs={{0,12},{4,8},{8,20},{12,16},{16,28},{20,24},{24,36},{28,32},{32,44... | collective-permute-start | bytes 786440 | tf_op jit(solution)/shard_map/ppermute | solution.py:302
  38.7 15.6 %collective-permute-start.6 = (f32[512,128]{1,0:T(8,128)}, f32[512,128]{1,0:T(8,128)S(1)}, u32[]{:S(2)}, u32[]{:S(2)}) collective-permute-start(f32[512,128]{1,0:T(8,128)} %bitcast_add_fusion.1.earlier.own), channel_id=1, source_target_pairs={{4,16},{12,24},{20,32},{28,40},{36,48},{44,56},{52,64},{60,72},{68... | collective-permute-start | bytes 786440 | tf_op jit(solution)/shard_map/ppermute | solution.py:303
  42.1 14.5 %collective-permute-start.11 = (f32[264,512]{1,0:T(8,128)}, f32[264,512]{1,0:T(8,128)}, u32[]{:S(2)}, u32[]{:S(2)}) collective-permute-start(f32[264,512]{1,0:T(8,128)} %get-tuple-element.19.near), channel_id=1, source_target_pairs={{0,4},{4,0},{8,12},{12,8},{16,20},{20,16},{24,28},{28,24},{32,36},... | collective-permute-start | bytes 1622024 | tf_op jit(solution)/shard_map/ppermute | solution.py:315
  45.0 1.9 %copy-start.9 = (f32[1,1,1536,512]{3,2,1,0:T(8,128)S(1)}, f32[1,1,1536,512]{3,2,1,0:T(8,128)}, u32[]{:S(2)}) copy-start(f32[1,1,1536,512]{3,2,1,0:T(8,128)} %u_ref.5) | copy-start | bytes 9437188
  46.9 8.8 %slice-start = ((f32[528,512]{1,0:T(8,128)}), f32[8,512]{1,0:T(8,128)S(1)}, s32[]{:S(2)}) async-start(f32[528,512]{1,0:T(8,128)} %copy-done.10), calls=%async_computation | async-start | bytes 32768 | tf_op jit(solution)/shard_map/slice | solution.py:317
  46.9 9.5 %copy-start.19 = (s32[1,1,8]{2,1,0:T(1,128)S(1)}, s32[1,1,8]{2,1,0:T(1,128)}, u32[]{:S(2)}) copy-start(s32[1,1,8]{2,1,0:T(1,128)} %param.14) | copy-start | bytes 100
  46.9 9.7 %copy-start.8 = (f32[264,512]{1,0:T(8,128)S(1)}, f32[264,512]{1,0:T(8,128)}, u32[]{:S(2)}) copy-start(f32[264,512]{1,0:T(8,128)} %get-tuple-element.19.near) | copy-start | bytes 1622020
  48.1 1.2 %copy-start.4 = (bf16[1536,512]{1,0:T(8,128)(2,1)}, bf16[1536,512]{1,0:T(8,128)(2,1)S(1)}, u32[]{:S(2)}) copy-start(bf16[1536,512]{1,0:T(8,128)(2,1)S(1)} %get-tuple-element.21.refs_9_.low) | copy-start | bytes 4718596
  49.4 17.0 %collective-permute-start.4 = (f32[512,128]{1,0:T(8,128)}, f32[512,128]{1,0:T(8,128)}, u32[]{:S(2)}, u32[]{:S(2)}) collective-permute-start(f32[512,128]{1,0:T(8,128)} %bitcast_add_fusion.1.earlier.own), channel_id=1, source_target_pairs={{0,4},{4,0},{8,12},{12,8},{16,20},{20,16},{24,28},{28,24},{32,36},... | collective-permute-start | bytes 786440 | tf_op jit(solution)/shard_map/ppermute | solution.py:330
  55.0 11.4 %collective-permute-start.7 = (f32[512,128]{1,0:T(8,128)}, f32[512,128]{1,0:T(8,128)S(1)}, u32[]{:S(2)}, u32[]{:S(2)}) collective-permute-start(f32[512,128]{1,0:T(8,128)} %after.2.near), channel_id=1, source_target_pairs={{0,4},{4,0},{8,12},{12,8},{16,20},{20,16},{24,28},{28,24},{32,36},... | collective-permute-start | bytes 786440 | tf_op jit(solution)/shard_map/ppermute | solution.py:329
  56.6 2.2 %copy-start.1 = (f32[2048,512]{1,0:T(8,128)S(1)}, f32[2048,512]{1,0:T(8,128)}, u32[]{:S(2)}) copy-start(f32[2048,512]{1,0:T(8,128)} %refs_7_.1) | copy-start | bytes 12582916
  58.8 1.4 %copy-start.5 = (bf16[1536,512]{1,0:T(8,128)(2,1)S(1)}, bf16[1536,512]{1,0:T(8,128)(2,1)}, u32[]{:S(2)}) copy-start(bf16[1536,512]{1,0:T(8,128)(2,1)} %copy-done.4) | copy-start | bytes 4718596
  60.2 1.2 %copy-start.11 = (f32[528,512]{1,0:T(8,128)S(1)}, f32[528,512]{1,0:T(8,128)}, u32[]{:S(2)}) copy-start(f32[528,512]{1,0:T(8,128)} %copy-done.10) | copy-start | bytes 3244036
  61.4 4.9 %copy-start.6 = (bf16[1536,512]{1,0:T(8,128)(2,1)S(1)}, bf16[1536,512]{1,0:T(8,128)(2,1)}, u32[]{:S(2)}) copy-start(bf16[1536,512]{1,0:T(8,128)(2,1)} %copy-done.4) | copy-start | bytes 4718596
  61.4 5.0 %copy-start.13 = (f32[512,128]{1,0:T(8,128)S(1)}, f32[512,128]{1,0:T(8,128)}, u32[]{:S(2)}) copy-start(f32[512,128]{1,0:T(8,128)} %copy-done.12) | copy-start | bytes 786436
  66.3 18.9 %copy-start.17 = (f32[1,1,512,128]{3,2,1,0:T(8,128)S(1)}, f32[1,1,512,128]{3,2,1,0:T(8,128)}, u32[]{:S(2)}) copy-start(f32[1,1,512,128]{3,2,1,0:T(8,128)} %param.17) | copy-start | bytes 786436
  69.0 10.0 %collective-permute-start.12 = (f32[512,128]{1,0:T(8,128)S(1)}, f32[512,128]{1,0:T(8,128)S(1)}, u32[]{:S(2)}, u32[]{:S(2)}) collective-permute-start(f32[512,128]{1,0:T(8,128)S(1)} %get-tuple-element.23), channel_id=1, source_target_pairs={{0,1},{1,2},{2,3},{3,0},{4,5},{5,6},{6,7},{7,4},{8,9},{9,10},{10,1... | collective-permute-start | bytes 786440 | tf_op jit(solution)/shard_map/ppermute | solution.py:260
  69.1 15.8 %collective-permute-start.13 = (f32[512,128]{1,0:T(8,128)S(1)}, f32[512,128]{1,0:T(8,128)S(1)}, u32[]{:S(2)}, u32[]{:S(2)}) collective-permute-start(f32[512,128]{1,0:T(8,128)S(1)} %get-tuple-element.24), channel_id=1, source_target_pairs={{0,2},{1,3},{2,0},{3,1},{4,6},{5,7},{6,4},{7,5},{8,10},{9,11},{10,... | collective-permute-start | bytes 786440 | tf_op jit(solution)/shard_map/ppermute | solution.py:260
  72.6 12.6 %collective-permute-start.14 = (f32[512,128]{1,0:T(8,128)S(1)}, f32[512,128]{1,0:T(8,128)S(1)}, u32[]{:S(2)}, u32[]{:S(2)}) collective-permute-start(f32[512,128]{1,0:T(8,128)S(1)} %get-tuple-element.25), channel_id=1, source_target_pairs={{0,3},{1,0},{2,1},{3,2},{4,7},{5,4},{6,5},{7,6},{8,11},{9,8},{10,9... | collective-permute-start | bytes 786440 | tf_op jit(solution)/shard_map/ppermute | solution.py:260
  (4 other events, 3.2 us)

commit v3 on v2

--- a/solution.py
+++ b/solution.py
@@ -171,6 +171,7 @@
         out_specs=ANY,
         out_shape=jax.ShapeDtypeStruct(array.shape, array.dtype),
         input_output_aliases={0: 0},
+        compiler_params=pltpu.CompilerParams(vmem_limit_bytes=1 << 20),
         cost_estimate=pl.CostEstimate(flops=1, bytes_accessed=1, transcendentals=0),
         name="after",
     )(array, earlier)
@@ -190,6 +191,7 @@
         out_shape=[jax.ShapeDtypeStruct(array.shape, F32), f32(SENT - HALF, W)],
         scratch_shapes=[pltpu.SemaphoreType.DMA],
         input_output_aliases={0: 0},
+        compiler_params=pltpu.CompilerParams(vmem_limit_bytes=1 << 20),
         cost_estimate=pl.CostEstimate(flops=1, bytes_accessed=1, transcendentals=0),
         name="take_marks",
     )(array)
@@ -278,7 +280,7 @@
     block = call(
         upper_rows_kernel, "upper_rows", (anc_a, parent, others_parent, where), [ANY, ANY], (top, u_a), f32(BLOCK, W),
         [pltpu.VMEM((SA, W), F32), pltpu.VMEM((SA, W), F32), pltpu.VMEM((W, W), F32),
-         pltpu.SemaphoreType.DMA((NA,)), pltpu.SemaphoreType.DMA((CHUNKS,))],
+         pltpu.SemaphoreType.DMA((NA,)), pltpu.SemaphoreType.DMA((CHUNKS,))], 58,
     )
     slabs_a = call(
         upper_sum_kernel, "upper_sum", (anc_a, where), [HELD, ANY], (block, u_a), [f32(W, TB)] * 4,

time: 87.1 us -> 81.8 us (0.939)
  local copies, waits for them, and re-layouts: 17.9 us -> 6.96 us
  starting transfers between devices: 24.2 us -> 26.8 us
  Pallas kernels: 16.8 us -> 18.7 us
    unnamed x41 -> x25, local copies, waits for them, and re-layouts: 17.1 us -> 5.44 us
    pallas_call x5, Pallas kernels: 15.5 us -> 18.7 us  [call(): pl.pallas_call(kernel, grid_spec=pltpu.PrefetchScalarGridSpec(num_scalar_...]
    ppermute x6, waiting for transfers between devices: 16.8 us -> 14.2 us  [to_owners(): arrived = [lax.ppermute(slabs[r], 'tile', ways[r]) for r in (2, 1, 3)]]
    ppermute x6, starting transfers between devices: 9.83 us -> 11.8 us  [to_owners(): arrived = [lax.ppermute(slabs[r], 'tile', ways[r]) for r in (2, 1, 3)]]
    ppermute x1, waiting for transfers between devices: 4.79 us -> 6.57 us  [body(): far_s = lax.ppermute(sigma_a, 'leaf', odd_on)]
    ppermute x1, waiting for transfers between devices: 0.01 us -> 1.57 us  [body(): near = lax.ppermute(latest, 'leaf', next_chip)]
    pallas_call x1, Pallas kernels: 1.32 us -> 0.02 us  [take_marks(): pl.pallas_call(take_marks_kernel, in_specs=[ANY], out_specs=[ANY, HELD],...]
    select_n x1, other arithmetic: 0.08 us -> 1.13 us  [body(): jnp.where(jnp.logical_xor(even, odd_heads), lax.dynamic_slice_in_dim(bloc...]
  transfers between devices with their start and end apart: 15 -> 15, of which waited for: 7 -> 7; matrix products, arithmetic and copies ran while one was open for 3% -> 5% of each run, Pallas kernels for 11% -> 11%
where the time goes in v3:
time: 81.8 us; the launch traced here: 80.4 us
  starting transfers between devices  26.8 us (33%)
  waiting for transfers between devices  22.9 us (28%)
  Pallas kernels  18.7 us (23%)
  local copies, waits for them, and re-layouts  6.96 us (9%)
  other arithmetic  2.82 us (3%)
  between operations  2.22 us (3%)
    pallas_call x5, Pallas kernels, call(): pl.pallas_call(kernel, grid_spec=pltpu.PrefetchScalarGridSpec(num_scalar_...  18.7 us
    ppermute x6, waiting for transfers between devices, to_owners(): arrived = [lax.ppermute(slabs[r], 'tile', ways[r]) for r in (2, 1, 3)]  14.2 us
    ppermute x6, starting transfers between devices, to_owners(): arrived = [lax.ppermute(slabs[r], 'tile', ways[r]) for r in (2, 1, 3)]  11.8 us
    ppermute x1, waiting for transfers between devices, body(): far_s = lax.ppermute(sigma_a, 'leaf', odd_on)  6.57 us
    unnamed x25, local copies, waits for them, and re-layouts  5.44 us
    ppermute x1, starting transfers between devices, body(): near_s = lax.ppermute(sigma_a, 'leaf', crossing)  5.24 us
    ppermute x1, starting transfers between devices, body(): near = lax.ppermute(latest, 'leaf', next_chip)  3.37 us
    ppermute x1, starting transfers between devices, body(): swapped = lax.ppermute(near, 'leaf', swap)  3 us
  transfers between devices with their start and end apart: 15, of which 7 were waited for; matrix products, arithmetic and copies ran while one was open for 5% of the time, Pallas kernels for 11%

profile of v3, /device:TPU:194, one launch (start us, length us, event | category | flops | bytes accessed | tf_op | source)
XLA Modules:
  0.0 80.4 jit_solution(16721808320425292511)
XLA Ops:
  1.4 0.6 pad_add_fusion.where
  2.0 7.8 %upper_rows.1.block.own = f32[528,512]{1,0:T(8,128)} custom-call(s32[1,12]{1,0:T(1,128)} %anc.3, s32[1]{0:T(128)} %copy.20.parent, s32[1]{0:T(128)} %collective-permute-done.others_parent, s32[3]{0:T(128)} %pad_add_fusion.where, f32[2048,512]{1,0:T(8,128)} %refs_7_.1, f32[1,1536,512]{2,1,0:T(8,128)} %u_ref.4), custom_call_target="tpu_custom_call" | custom-call | flops 1048576 | bytes 65536 | tf_op jit(solution)/shard_map/upper_rows/pallas_call | solution.py:49
  9.8 0.6 collective-permute-start.8
  10.3 1.3 %collective-permute-start.9 = (f32[528,512]{1,0:T(8,128)}, f32[528,512]{1,0:T(8,128)}, u32[]{:S(2)}, u32[]{:S(2)}) collective-permute-start(f32[528,512]{1,0:T(8,128)} %upper_rows.1.block.own), channel_id=1, source_target_pairs={{4,16},{12,24},{20,32},{28,40},{36,48},{44,56},{52,64},{60,72},{68... | collective-permute-start | bytes 3244040 | tf_op jit(solution)/shard_map/ppermute | solution.py:297
  12.4 1.2 %copy-done.1 = f32[528,512]{1,0:T(8,128)S(1)} copy-done((f32[528,512]{1,0:T(8,128)S(1)}, f32[528,512]{1,0:T(8,128)}, u32[]{:S(2)}) %copy-start.1) | copy-done | bytes 1081368
  13.6 2.0 %upper_sum.1 = (f32[512,128]{1,0:T(8,128)S(1)}, f32[512,128]{1,0:T(8,128)S(1)}, f32[512,128]{1,0:T(8,128)S(1)}, f32[512,128]{1,0:T(8,128)S(1)}) custom-call(s32[1,12]{1,0:T(1,128)S(1)} %copy-done.7, s32[3]{0:T(128)S(1)} %copy-done.6, f32[528,512]{1,0:T(8,128)S(1)} %copy-done.1, f32[1,1536,512]{2,1,0:T(8,128)S(1)} %copy-done.3), custom_call_target="tpu_custom_call" | custom-call | flops 1048576 | bytes 65536 | tf_op jit(solution)/shard_map/upper_sum/pallas_call | solution.py:49
  15.6 1.7 %collective-permute-start.1 = (f32[512,128]{1,0:T(8,128)S(1)}, f32[512,128]{1,0:T(8,128)S(1)}, u32[]{:S(2)}, u32[]{:S(2)}) collective-permute-start(f32[512,128]{1,0:T(8,128)S(1)} %get-tuple-element.15), channel_id=1, source_target_pairs={{0,1},{1,2},{2,3},{3,0},{4,5},{5,6},{6,7},{7,4},{8,9},{9,10},{10,1... | collective-permute-start | bytes 786440 | tf_op jit(solution)/shard_map/ppermute | solution.py:262
  17.3 2.9 %collective-permute-start.2 = (f32[512,128]{1,0:T(8,128)S(1)}, f32[512,128]{1,0:T(8,128)S(1)}, u32[]{:S(2)}, u32[]{:S(2)}) collective-permute-start(f32[512,128]{1,0:T(8,128)S(1)} %get-tuple-element.16), channel_id=1, source_target_pairs={{0,2},{1,3},{2,0},{3,1},{4,6},{5,7},{6,4},{7,5},{8,10},{9,11},{10,... | collective-permute-start | bytes 786440 | tf_op jit(solution)/shard_map/ppermute | solution.py:262
  20.1 1.4 %collective-permute-start.3 = (f32[512,128]{1,0:T(8,128)S(1)}, f32[512,128]{1,0:T(8,128)S(1)}, u32[]{:S(2)}, u32[]{:S(2)}) collective-permute-start(f32[512,128]{1,0:T(8,128)S(1)} %get-tuple-element.17), channel_id=1, source_target_pairs={{0,3},{1,0},{2,1},{3,2},{4,7},{5,4},{6,5},{7,6},{8,11},{9,8},{10,9... | collective-permute-start | bytes 786440 | tf_op jit(solution)/shard_map/ppermute | solution.py:262
  21.5 1.1 %dynamic-slice_select_fusion = f32[264,512]{1,0:T(8,128)S(1)} fusion(f32[528,512]{1,0:T(8,128)} %collective-permute-done.8.other, s32[]{:T(128)S(6)} %select_n.87, f32[528,512]{1,0:T(8,128)S(1)} %copy-done.1, pred[]{:T(512)S(6)} %xor.3), kind=kLoop, calls=%fused_computation | loop fusion | flops 135168 | bytes 1622021 | tf_op jit(solution)/shard_map/jit(_where)/select_n | solution.py:291
  22.7 3.4 %collective-permute-start.10 = (f32[264,512]{1,0:T(8,128)S(1)}, f32[264,512]{1,0:T(8,128)S(1)}, u32[]{:S(2)}, u32[]{:S(2)}) collective-permute-start(f32[264,512]{1,0:T(8,128)S(1)} %dynamic-slice_select_fusion), channel_id=1, source_target_pairs={{0,8},{4,12},{8,16},{12,20},{16,24},{20,28},{24,32},{28,36},{32,40... | collective-permute-start | bytes 1622024 | tf_op jit(solution)/shard_map/ppermute | solution.py:296
  26.0 3.9 %collective-permute-done.2 = f32[512,128]{1,0:T(8,128)S(1)} collective-permute-done((f32[512,128]{1,0:T(8,128)S(1)}, f32[512,128]{1,0:T(8,128)S(1)}, u32[]{:S(2)}, u32[]{:S(2)}) %collective-permute-start.2) | collective-permute-done | bytes 262176 | tf_op jit(solution)/shard_map/ppermute | solution.py:262
  30.0 0.5 collective-permute-done.3
  30.6 5.2 %collective-permute-start.5 = (f32[512,128]{1,0:T(8,128)S(1)}, f32[512,128]{1,0:T(8,128)S(1)}, u32[]{:S(2)}, u32[]{:S(2)}) collective-permute-start(f32[512,128]{1,0:T(8,128)S(1)} %bitcast_add_fusion.1.earlier.own), channel_id=1, source_target_pairs={{0,12},{4,8},{8,20},{12,16},{16,28},{20,24},{24,36},{28,32},{32,44... | collective-permute-start | bytes 786440 | tf_op jit(solution)/shard_map/ppermute | solution.py:304
  35.8 1.3 %collective-permute-start.6 = (f32[512,128]{1,0:T(8,128)S(1)}, f32[512,128]{1,0:T(8,128)S(1)}, u32[]{:S(2)}, u32[]{:S(2)}) collective-permute-start(f32[512,128]{1,0:T(8,128)S(1)} %bitcast_add_fusion.1.earlier.own), channel_id=1, source_target_pairs={{4,16},{12,24},{20,32},{28,40},{36,48},{44,56},{52,64},{60,72},{68... | collective-permute-start | bytes 786440 | tf_op jit(solution)/shard_map/ppermute | solution.py:305
  37.1 1.6 %collective-permute-done.10.array = f32[264,512]{1,0:T(8,128)S(1)} collective-permute-done((f32[264,512]{1,0:T(8,128)S(1)}, f32[264,512]{1,0:T(8,128)S(1)}, u32[]{:S(2)}, u32[]{:S(2)}) %collective-permute-start.10) | collective-permute-done | bytes 540704 | tf_op jit(solution)/shard_map/ppermute | solution.py:296
  38.7 3.0 %collective-permute-start.11 = (f32[264,512]{1,0:T(8,128)S(1)}, f32[264,512]{1,0:T(8,128)S(1)}, u32[]{:S(2)}, u32[]{:S(2)}) collective-permute-start(f32[264,512]{1,0:T(8,128)S(1)} %get-tuple-element.19.near), channel_id=1, source_target_pairs={{0,4},{4,0},{8,12},{12,8},{16,20},{20,16},{24,28},{28,24},{32,36},... | collective-permute-start | bytes 1622024 | tf_op jit(solution)/shard_map/ppermute | solution.py:317
  41.9 1.9 %copy-done.4 = f32[1,1,1536,512]{3,2,1,0:T(8,128)S(1)} copy-done((f32[1,1,1536,512]{3,2,1,0:T(8,128)S(1)}, f32[1,1,1536,512]{3,2,1,0:T(8,128)}, u32[]{:S(2)}) %copy-start.4) | copy-done | bytes 3145752
  43.8 1.2 %lower_prepare.1 = (bf16[1536,512]{1,0:T(8,128)(2,1)S(1)}, bf16[1536,512]{1,0:T(8,128)(2,1)S(1)}) custom-call(s32[48]{0:T(128)S(1)} %reshape.8.pattern, f32[1,1,1536,512]{3,2,1,0:T(8,128)S(1)} %copy-done.4), custom_call_target="tpu_custom_call" | custom-call | flops 1048576 | bytes 65536 | tf_op jit(solution)/shard_map/lower_prepare/pallas_call | solution.py:49
  45.2 0.5 collective-permute-done.5.array
  45.7 6.6 %collective-permute-done.6.earlier.far = f32[512,128]{1,0:T(8,128)S(1)} collective-permute-done((f32[512,128]{1,0:T(8,128)S(1)}, f32[512,128]{1,0:T(8,128)S(1)}, u32[]{:S(2)}, u32[]{:S(2)}) %collective-permute-start.6) | collective-permute-done | bytes 262176 | tf_op jit(solution)/shard_map/ppermute | solution.py:305
  52.3 0.7 slice.17
  53.0 0.7 slice.18
  54.0 2.2 %copy-done = f32[2048,512]{1,0:T(8,128)S(1)} copy-done((f32[2048,512]{1,0:T(8,128)S(1)}, f32[2048,512]{1,0:T(8,128)}, u32[]{:S(2)}) %copy-start) | copy-done | bytes 4194328
  56.2 6.0 %lower_cross.1.p_ref = f32[512,512]{1,0:T(8,128)S(1)} custom-call(s32[2]{0:T(128)S(1)} %pad_add_fusion.1.code, s32[3]{0:T(128)S(1)} %copy-done.6, s32[8]{0:T(128)S(1)} %select_reduce_fusion.far_tiles, f32[528,512]{1,0:T(8,128)S(1)} %copy-done.2, f32[528,512]{1,0:T(8,128)} %collective-permute-done.8.other, f32[264,512]{1,0:T(8,128)S(1)} %get-tuple-element.19.near, ...), custom_call_target="tpu_custom_call" | custom-call | flops 1048576 | bytes 65536 | tf_op jit(solution)/shard_map/lower_cross/pallas_call | solution.py:49
  62.2 1.7 %lower_sum.1 = (f32[512,128]{1,0:T(8,128)S(1)}, f32[512,128]{1,0:T(8,128)S(1)}, f32[512,128]{1,0:T(8,128)S(1)}, f32[512,128]{1,0:T(8,128)S(1)}) custom-call(s32[2]{0:T(128)S(1)} %pad_add_fusion.1.code, s32[3]{0:T(128)S(1)} %copy-done.6, f32[512,128]{1,0:T(8,128)S(1)} %bitcast_add_fusion.1.earlier.own, f32[512,128]{1,0:T(8,128)S(1)} %collective-permute-done.4.even, ...), custom_call_target="tpu_custom_call" | custom-call | flops 1048576 | bytes 65536 | tf_op jit(solution)/shard_map/lower_sum/pallas_call | solution.py:49
  64.0 1.6 %collective-permute-start.12 = (f32[512,128]{1,0:T(8,128)S(1)}, f32[512,128]{1,0:T(8,128)S(1)}, u32[]{:S(2)}, u32[]{:S(2)}) collective-permute-start(f32[512,128]{1,0:T(8,128)S(1)} %get-tuple-element.23), channel_id=1, source_target_pairs={{0,1},{1,2},{2,3},{3,0},{4,5},{5,6},{6,7},{7,4},{8,9},{9,10},{10,1... | collective-permute-start | bytes 786440 | tf_op jit(solution)/shard_map/ppermute | solution.py:262
  65.6 2.8 %collective-permute-start.13 = (f32[512,128]{1,0:T(8,128)S(1)}, f32[512,128]{1,0:T(8,128)S(1)}, u32[]{:S(2)}, u32[]{:S(2)}) collective-permute-start(f32[512,128]{1,0:T(8,128)S(1)} %get-tuple-element.24), channel_id=1, source_target_pairs={{0,2},{1,3},{2,0},{3,1},{4,6},{5,7},{6,4},{7,5},{8,10},{9,11},{10,... | collective-permute-start | bytes 786440 | tf_op jit(solution)/shard_map/ppermute | solution.py:262
  68.4 1.5 %collective-permute-start.14 = (f32[512,128]{1,0:T(8,128)S(1)}, f32[512,128]{1,0:T(8,128)S(1)}, u32[]{:S(2)}, u32[]{:S(2)}) collective-permute-start(f32[512,128]{1,0:T(8,128)S(1)} %get-tuple-element.25), channel_id=1, source_target_pairs={{0,3},{1,0},{2,1},{3,2},{4,7},{5,4},{6,5},{7,6},{8,11},{9,8},{10,9... | collective-permute-start | bytes 786440 | tf_op jit(solution)/shard_map/ppermute | solution.py:262
  69.9 3.5 %collective-permute-done.12 = f32[512,128]{1,0:T(8,128)S(1)} collective-permute-done((f32[512,128]{1,0:T(8,128)S(1)}, f32[512,128]{1,0:T(8,128)S(1)}, u32[]{:S(2)}, u32[]{:S(2)}) %collective-permute-start.12) | collective-permute-done | bytes 262176 | tf_op jit(solution)/shard_map/ppermute | solution.py:262
  73.4 6.2 %collective-permute-done.13 = f32[512,128]{1,0:T(8,128)S(1)} collective-permute-done((f32[512,128]{1,0:T(8,128)S(1)}, f32[512,128]{1,0:T(8,128)S(1)}, u32[]{:S(2)}, u32[]{:S(2)}) %collective-permute-start.13) | collective-permute-done | bytes 262176 | tf_op jit(solution)/shard_map/ppermute | solution.py:262
  79.6 0.8 bitcast_add_fusion
  (42 shorter events, 0.8 us)
Async XLA Ops:
  0.6 1.3 %collective-permute-start = (s32[1]{0:T(128)}, s32[1]{0:T(128)}, u32[]{:S(2)}, u32[]{:S(2)}) collective-permute-start(s32[1]{0:T(128)} %param.13), channel_id=1, source_target_pairs={{0,4},{4,0},{8,12},{12,8},{16,20},{20,16},{24,28},{28,24},{32,36},... | collective-permute-start | bytes 20 | tf_op jit(solution)/shard_map/ppermute | solution.py:279
  1.9 10.4 %copy-start.6 = (s32[3]{0:T(128)S(1)}, s32[3]{0:T(128)}, u32[]{:S(2)}) copy-start(s32[3]{0:T(128)} %pad_add_fusion.where) | copy-start | bytes 40
  1.9 10.4 %copy-start.7 = (s32[1,12]{1,0:T(1,128)S(1)}, s32[1,12]{1,0:T(1,128)}, u32[]{:S(2)}) copy-start(s32[1,12]{1,0:T(1,128)} %anc.3) | copy-start | bytes 148
  2.0 10.4 %copy-start.3 = (f32[1,1536,512]{2,1,0:T(8,128)S(1)}, f32[1,1536,512]{2,1,0:T(8,128)}, u32[]{:S(2)}) copy-start(f32[1,1536,512]{2,1,0:T(8,128)} %u_ref.4) | copy-start | bytes 9437188
  9.8 11.8 %collective-permute-start.8 = (f32[528,512]{1,0:T(8,128)}, f32[528,512]{1,0:T(8,128)}, u32[]{:S(2)}, u32[]{:S(2)}) collective-permute-start(f32[528,512]{1,0:T(8,128)} %upper_rows.1.block.own), channel_id=1, source_target_pairs={{0,4},{4,0},{8,12},{12,8},{16,20},{20,16},{24,28},{28,24},{32,36},... | collective-permute-start | bytes 3244040 | tf_op jit(solution)/shard_map/ppermute | solution.py:289
  10.3 42.7 %collective-permute-start.9 = (f32[528,512]{1,0:T(8,128)}, f32[528,512]{1,0:T(8,128)}, u32[]{:S(2)}, u32[]{:S(2)}) collective-permute-start(f32[528,512]{1,0:T(8,128)} %upper_rows.1.block.own), channel_id=1, source_target_pairs={{4,16},{12,24},{20,32},{28,40},{36,48},{44,56},{52,64},{60,72},{68... | collective-permute-start | bytes 3244040 | tf_op jit(solution)/shard_map/ppermute | solution.py:297
  12.3 1.2 %copy-start.1 = (f32[528,512]{1,0:T(8,128)S(1)}, f32[528,512]{1,0:T(8,128)}, u32[]{:S(2)}) copy-start(f32[528,512]{1,0:T(8,128)} %upper_rows.1.block.own) | copy-start | bytes 3244036
  15.6 14.9 %copy-start.8 = (f32[1,512,128]{2,1,0:T(8,128)S(1)}, f32[1,512,128]{2,1,0:T(8,128)}, u32[]{:S(2)}) copy-start(f32[1,512,128]{2,1,0:T(8,128)} %param.12) | copy-start | bytes 786436
  15.6 10.5 %collective-permute-start.1 = (f32[512,128]{1,0:T(8,128)S(1)}, f32[512,128]{1,0:T(8,128)S(1)}, u32[]{:S(2)}, u32[]{:S(2)}) collective-permute-start(f32[512,128]{1,0:T(8,128)S(1)} %get-tuple-element.15), channel_id=1, source_target_pairs={{0,1},{1,2},{2,3},{3,0},{4,5},{5,6},{6,7},{7,4},{8,9},{9,10},{10,1... | collective-permute-start | bytes 786440 | tf_op jit(solution)/shard_map/ppermute | solution.py:262
  17.3 12.7 %collective-permute-start.2 = (f32[512,128]{1,0:T(8,128)S(1)}, f32[512,128]{1,0:T(8,128)S(1)}, u32[]{:S(2)}, u32[]{:S(2)}) collective-permute-start(f32[512,128]{1,0:T(8,128)S(1)} %get-tuple-element.16), channel_id=1, source_target_pairs={{0,2},{1,3},{2,0},{3,1},{4,6},{5,7},{6,4},{7,5},{8,10},{9,11},{10,... | collective-permute-start | bytes 786440 | tf_op jit(solution)/shard_map/ppermute | solution.py:262
  20.1 10.4 %collective-permute-start.3 = (f32[512,128]{1,0:T(8,128)S(1)}, f32[512,128]{1,0:T(8,128)S(1)}, u32[]{:S(2)}, u32[]{:S(2)}) collective-permute-start(f32[512,128]{1,0:T(8,128)S(1)} %get-tuple-element.17), channel_id=1, source_target_pairs={{0,3},{1,0},{2,1},{3,2},{4,7},{5,4},{6,5},{7,6},{8,11},{9,8},{10,9... | collective-permute-start | bytes 786440 | tf_op jit(solution)/shard_map/ppermute | solution.py:262
  22.7 16.0 %collective-permute-start.10 = (f32[264,512]{1,0:T(8,128)S(1)}, f32[264,512]{1,0:T(8,128)S(1)}, u32[]{:S(2)}, u32[]{:S(2)}) collective-permute-start(f32[264,512]{1,0:T(8,128)S(1)} %dynamic-slice_select_fusion), channel_id=1, source_target_pairs={{0,8},{4,12},{8,16},{12,20},{16,24},{20,28},{24,32},{28,36},{32,40... | collective-permute-start | bytes 1622024 | tf_op jit(solution)/shard_map/ppermute | solution.py:296
  30.5 11.2 %copy-start.10 = (s32[1,1,12,4]{2,3,1,0:T(4,128)S(1)}, s32[1,1,12,4]{2,3,1,0:T(4,128)}, u32[]{:S(2)}) copy-start(s32[1,1,12,4]{2,3,1,0:T(4,128)} %param.15) | copy-start | bytes 580
  30.6 31.7 %copy-start.5 = (f32[512,128]{1,0:T(8,128)}, f32[512,128]{1,0:T(8,128)S(1)}, u32[]{:S(2)}) copy-start(f32[512,128]{1,0:T(8,128)S(1)} %bitcast_add_fusion.1.earlier.own) | copy-start | bytes 786436
  30.6 15.2 %collective-permute-start.5 = (f32[512,128]{1,0:T(8,128)S(1)}, f32[512,128]{1,0:T(8,128)S(1)}, u32[]{:S(2)}, u32[]{:S(2)}) collective-permute-start(f32[512,128]{1,0:T(8,128)S(1)} %bitcast_add_fusion.1.earlier.own), channel_id=1, source_target_pairs={{0,12},{4,8},{8,20},{12,16},{16,28},{20,24},{24,36},{28,32},{32,44... | collective-permute-start | bytes 786440 | tf_op jit(solution)/shard_map/ppermute | solution.py:304
  35.8 16.5 %collective-permute-start.6 = (f32[512,128]{1,0:T(8,128)S(1)}, f32[512,128]{1,0:T(8,128)S(1)}, u32[]{:S(2)}, u32[]{:S(2)}) collective-permute-start(f32[512,128]{1,0:T(8,128)S(1)} %bitcast_add_fusion.1.earlier.own), channel_id=1, source_target_pairs={{4,16},{12,24},{20,32},{28,40},{36,48},{44,56},{52,64},{60,72},{68... | collective-permute-start | bytes 786440 | tf_op jit(solution)/shard_map/ppermute | solution.py:305
  38.7 15.2 %collective-permute-start.11 = (f32[264,512]{1,0:T(8,128)S(1)}, f32[264,512]{1,0:T(8,128)S(1)}, u32[]{:S(2)}, u32[]{:S(2)}) collective-permute-start(f32[264,512]{1,0:T(8,128)S(1)} %get-tuple-element.19.near), channel_id=1, source_target_pairs={{0,4},{4,0},{8,12},{12,8},{16,20},{20,16},{24,28},{28,24},{32,36},... | collective-permute-start | bytes 1622024 | tf_op jit(solution)/shard_map/ppermute | solution.py:317
  41.9 1.9 %copy-start.4 = (f32[1,1,1536,512]{3,2,1,0:T(8,128)S(1)}, f32[1,1,1536,512]{3,2,1,0:T(8,128)}, u32[]{:S(2)}) copy-start(f32[1,1,1536,512]{3,2,1,0:T(8,128)} %u_ref.5) | copy-start | bytes 9437188
  43.8 1.3 %copy-start.2 = (f32[528,512]{1,0:T(8,128)S(1)}, f32[528,512]{1,0:T(8,128)}, u32[]{:S(2)}) copy-start(f32[528,512]{1,0:T(8,128)} %upper_rows.1.block.own) | copy-start | bytes 3244036
  43.8 10.0 %copy-start.11 = (s32[1,1,8]{2,1,0:T(1,128)S(1)}, s32[1,1,8]{2,1,0:T(1,128)}, u32[]{:S(2)}) copy-start(s32[1,1,8]{2,1,0:T(1,128)} %param.14) | copy-start | bytes 100
  45.1 17.1 %collective-permute-start.4 = (f32[512,128]{1,0:T(8,128)S(1)}, f32[512,128]{1,0:T(8,128)S(1)}, u32[]{:S(2)}, u32[]{:S(2)}) collective-permute-start(f32[512,128]{1,0:T(8,128)S(1)} %bitcast_add_fusion.1.earlier.own), channel_id=1, source_target_pairs={{0,4},{4,0},{8,12},{12,8},{16,20},{20,16},{24,28},{28,24},{32,36},... | collective-permute-start | bytes 786440 | tf_op jit(solution)/shard_map/ppermute | solution.py:332
  52.3 9.9 %collective-permute-start.7 = (f32[512,128]{1,0:T(8,128)S(1)}, f32[512,128]{1,0:T(8,128)S(1)}, u32[]{:S(2)}, u32[]{:S(2)}) collective-permute-start(f32[512,128]{1,0:T(8,128)S(1)} %after.2.near), channel_id=1, source_target_pairs={{0,4},{4,0},{8,12},{12,8},{16,20},{20,16},{24,28},{28,24},{32,36},... | collective-permute-start | bytes 786440 | tf_op jit(solution)/shard_map/ppermute | solution.py:331
  54.0 2.2 %copy-start = (f32[2048,512]{1,0:T(8,128)S(1)}, f32[2048,512]{1,0:T(8,128)}, u32[]{:S(2)}) copy-start(f32[2048,512]{1,0:T(8,128)} %refs_7_.1) | copy-start | bytes 12582916
  62.2 17.4 %copy-start.9 = (f32[1,1,512,128]{3,2,1,0:T(8,128)S(1)}, f32[1,1,512,128]{3,2,1,0:T(8,128)}, u32[]{:S(2)}) copy-start(f32[1,1,512,128]{3,2,1,0:T(8,128)} %param.17) | copy-start | bytes 786436
  64.0 9.4 %collective-permute-start.12 = (f32[512,128]{1,0:T(8,128)S(1)}, f32[512,128]{1,0:T(8,128)S(1)}, u32[]{:S(2)}, u32[]{:S(2)}) collective-permute-start(f32[512,128]{1,0:T(8,128)S(1)} %get-tuple-element.23), channel_id=1, source_target_pairs={{0,1},{1,2},{2,3},{3,0},{4,5},{5,6},{6,7},{7,4},{8,9},{9,10},{10,1... | collective-permute-start | bytes 786440 | tf_op jit(solution)/shard_map/ppermute | solution.py:262
  65.6 14.1 %collective-permute-start.13 = (f32[512,128]{1,0:T(8,128)S(1)}, f32[512,128]{1,0:T(8,128)S(1)}, u32[]{:S(2)}, u32[]{:S(2)}) collective-permute-start(f32[512,128]{1,0:T(8,128)S(1)} %get-tuple-element.24), channel_id=1, source_target_pairs={{0,2},{1,3},{2,0},{3,1},{4,6},{5,7},{6,4},{7,5},{8,10},{9,11},{10,... | collective-permute-start | bytes 786440 | tf_op jit(solution)/shard_map/ppermute | solution.py:262
  68.4 11.2 %collective-permute-start.14 = (f32[512,128]{1,0:T(8,128)S(1)}, f32[512,128]{1,0:T(8,128)S(1)}, u32[]{:S(2)}, u32[]{:S(2)}) collective-permute-start(f32[512,128]{1,0:T(8,128)S(1)} %get-tuple-element.25), channel_id=1, source_target_pairs={{0,3},{1,0},{2,1},{3,2},{4,7},{5,4},{6,5},{7,6},{8,11},{9,8},{10,9... | collective-permute-start | bytes 786440 | tf_op jit(solution)/shard_map/ppermute | solution.py:262

commit v4 on v3

--- a/solution.py
+++ b/solution.py
@@ -30,10 +30,9 @@
 
 
 def dot3(a, b, contract):
-    def one(u, v):
-        return lax.dot_general(u, v, (contract, ((), ())), preferred_element_type=F32)
-
-    return one(a[0], b[0]) + (one(a[0], b[1]) + one(a[1], b[0]))
+    left = jnp.concatenate([a[0], a[0], a[1]], axis=contract[0][0])
+    right = jnp.concatenate([b[0], b[1], b[0]], axis=contract[1][0])
+    return lax.dot_general(left, right, (contract, ((), ())), preferred_element_type=F32)
 
 
 HELD = pl.BlockSpec(memory_space=pltpu.VMEM)
@@ -280,7 +279,7 @@
     block = call(
         upper_rows_kernel, "upper_rows", (anc_a, parent, others_parent, where), [ANY, ANY], (top, u_a), f32(BLOCK, W),
         [pltpu.VMEM((SA, W), F32), pltpu.VMEM((SA, W), F32), pltpu.VMEM((W, W), F32),
-         pltpu.SemaphoreType.DMA((NA,)), pltpu.SemaphoreType.DMA((CHUNKS,))], 58,
+         pltpu.SemaphoreType.DMA((NA,)), pltpu.SemaphoreType.DMA((CHUNKS,))], 48,
     )
     slabs_a = call(
         upper_sum_kernel, "upper_sum", (anc_a, where), [HELD, ANY], (block, u_a), [f32(W, TB)] * 4,
@@ -315,8 +314,9 @@
 
     near, near_marks = take_marks(after(near, sigma_a))
     swapped = lax.ppermute(near, "leaf", swap)
+    own_marks = jnp.pad(anc_a.astype(F32), ((0, 0), (0, W - NA)))
     marked = jnp.where(
-        code_x == 0, block[HALF:SENT], jnp.where(code_x == 1, other[HALF:SENT], jnp.where(code_x == 3, far[HALF:SENT], near_marks))
+        code_x == 0, own_marks, jnp.where(code_x == 1, other[HALF:SENT], jnp.where(code_x == 3, far[HALF:SENT], near_marks))
     )[0, :NA].astype(jnp.int32)
     far_tiles = jnp.sum(
         jnp.where(sel_b[0, 0][:, None] == jnp.arange(NA, dtype=jnp.int32)[None], marked[None], 0), axis=1

time: 81.8 us -> 80.7 us (0.987); the launches traced: 80.4 us -> 80.2 us
  Pallas kernels: 18.7 us -> 15.9 us
  waiting for transfers between devices: 22.9 us -> 25.4 us
  local copies, waits for them, and re-layouts: 6.96 us -> 9.44 us
  other arithmetic: 2.82 us -> 1.28 us
    unnamed x25 -> x23, local copies, waits for them, and re-layouts: 5.44 us -> 8.62 us
    pallas_call x5, Pallas kernels: 18.7 us -> 15.9 us  [call(): pl.pallas_call(kernel, grid_spec=pltpu.PrefetchScalarGridSpec(num_scalar_...]
    ppermute x6, waiting for transfers between devices: 14.2 us -> 16.5 us  [to_owners(): arrived = [lax.ppermute(slabs[r], 'tile', ways[r]) for r in (2, 1, 3)]]
    select_n x1, other arithmetic: 1.13 us -> 0.08 us  [body(): jnp.where(jnp.logical_xor(even, odd_heads), lax.dynamic_slice_in_dim(bloc...]
  transfers between devices with their start and end apart: 15 -> 15, of which waited for: 7 -> 8; matrix products, arithmetic and copies ran while one was open for 5% -> 2% of each run, Pallas kernels for 11% -> 11%
where the time goes in v4:
time: 80.7 us; the launch traced here: 80.2 us
  starting transfers between devices  26 us (32%)
  waiting for transfers between devices  25.4 us (31%)
  Pallas kernels  15.9 us (20%)
  local copies, waits for them, and re-layouts  9.44 us (12%)
  between operations  2.11 us (3%)
  other arithmetic  1.28 us (2%)
    ppermute x6, waiting for transfers between devices, to_owners(): arrived = [lax.ppermute(slabs[r], 'tile', ways[r]) for r in (2, 1, 3)]  16.5 us
    pallas_call x5, Pallas kernels, call(): pl.pallas_call(kernel, grid_spec=pltpu.PrefetchScalarGridSpec(num_scalar_...  15.9 us
    ppermute x6, starting transfers between devices, to_owners(): arrived = [lax.ppermute(slabs[r], 'tile', ways[r]) for r in (2, 1, 3)]  11.9 us
    unnamed x23, local copies, waits for them, and re-layouts  8.62 us
    ppermute x1, waiting for transfers between devices, body(): far_s = lax.ppermute(sigma_a, 'leaf', odd_on)  6.39 us
    ppermute x1, starting transfers between devices, body(): near_s = lax.ppermute(sigma_a, 'leaf', crossing)  5.22 us
    ppermute x1, starting transfers between devices, body(): near = lax.ppermute(latest, 'leaf', next_chip)  3.36 us
    ppermute x1, starting transfers between devices, body(): swapped = lax.ppermute(near, 'leaf', swap)  2.47 us
  transfers between devices with their start and end apart: 15, of which 8 were waited for; matrix products, arithmetic and copies ran while one was open for 2% of the time, Pallas kernels for 11%

profile of v4, /device:TPU:194, one launch (start us, length us, event | category | flops | bytes accessed | tf_op | source)
XLA Modules:
  0.0 80.2 jit_solution(11118192064923180419)
XLA Ops:
  1.5 0.6 collective-permute-done.others_parent
  2.1 1.9 %copy-done.1 = f32[1,1536,512]{2,1,0:T(8,128)S(1)} copy-done((f32[1,1536,512]{2,1,0:T(8,128)S(1)}, f32[1,1536,512]{2,1,0:T(8,128)}, u32[]{:S(2)}) %copy-start.1) | copy-done | bytes 3145752
  4.0 0.7 copy-done.5
  4.7 5.5 %upper_rows.1.block.own = f32[528,512]{1,0:T(8,128)S(1)} custom-call(s32[1,12]{1,0:T(1,128)S(1)} %copy-done.5, s32[1]{0:T(128)} %copy.20.parent, s32[1]{0:T(128)} %collective-permute-done.others_parent, s32[3]{0:T(128)S(1)} %pad_add_fusion.where, f32[2048,512]{1,0:T(8,128)} %refs_7_.1, f32[1,1536,512]{2,1,0:T(8,128)S(1)} %copy-done.1), custom_call_target="tpu_custom_call" | custom-call | flops 1048576 | bytes 65536 | tf_op jit(solution)/shard_map/upper_rows/pallas_call | solution.py:48
  10.1 0.3 collective-permute-start.8
  10.4 1.3 %collective-permute-start.9 = (f32[528,512]{1,0:T(8,128)S(1)}, f32[528,512]{1,0:T(8,128)}, u32[]{:S(2)}, u32[]{:S(2)}) collective-permute-start(f32[528,512]{1,0:T(8,128)S(1)} %upper_rows.1.block.own), channel_id=1, source_target_pairs={{4,16},{12,24},{20,32},{28,40},{36,48},{44,56},{52,64},{60,72},{68... | collective-permute-start | bytes 3244040 | tf_op jit(solution)/shard_map/ppermute | solution.py:296
  12.3 1.9 %copy-done.2 = f32[1,1536,512]{2,1,0:T(8,128)S(1)} copy-done((f32[1,1536,512]{2,1,0:T(8,128)S(1)}, f32[1,1536,512]{2,1,0:T(8,128)}, u32[]{:S(2)}) %copy-start.2) | copy-done | bytes 3145752
  14.2 1.9 %upper_sum.1 = (f32[512,128]{1,0:T(8,128)S(1)}, f32[512,128]{1,0:T(8,128)S(1)}, f32[512,128]{1,0:T(8,128)S(1)}, f32[512,128]{1,0:T(8,128)S(1)}) custom-call(s32[1,12]{1,0:T(1,128)S(1)} %copy-done.6, s32[3]{0:T(128)S(1)} %pad_add_fusion.where, f32[528,512]{1,0:T(8,128)S(1)} %upper_rows.1.block.own, f32[1,1536,512]{2,1,0:T(8,128)S(1)} %copy-done.2), custom_call_target="tpu_custom_call" | custom-call | flops 1048576 | bytes 65536 | tf_op jit(solution)/shard_map/upper_sum/pallas_call | solution.py:48
  16.2 1.7 %collective-permute-start.1 = (f32[512,128]{1,0:T(8,128)S(1)}, f32[512,128]{1,0:T(8,128)S(1)}, u32[]{:S(2)}, u32[]{:S(2)}) collective-permute-start(f32[512,128]{1,0:T(8,128)S(1)} %get-tuple-element.15), channel_id=1, source_target_pairs={{0,1},{1,2},{2,3},{3,0},{4,5},{5,6},{6,7},{7,4},{8,9},{9,10},{10,1... | collective-permute-start | bytes 786440 | tf_op jit(solution)/shard_map/ppermute | solution.py:261
  17.8 2.9 %collective-permute-start.2 = (f32[512,128]{1,0:T(8,128)S(1)}, f32[512,128]{1,0:T(8,128)S(1)}, u32[]{:S(2)}, u32[]{:S(2)}) collective-permute-start(f32[512,128]{1,0:T(8,128)S(1)} %get-tuple-element.16), channel_id=1, source_target_pairs={{0,2},{1,3},{2,0},{3,1},{4,6},{5,7},{6,4},{7,5},{8,10},{9,11},{10,... | collective-permute-start | bytes 786440 | tf_op jit(solution)/shard_map/ppermute | solution.py:261
  20.7 1.4 %collective-permute-start.3 = (f32[512,128]{1,0:T(8,128)S(1)}, f32[512,128]{1,0:T(8,128)S(1)}, u32[]{:S(2)}, u32[]{:S(2)}) collective-permute-start(f32[512,128]{1,0:T(8,128)S(1)} %get-tuple-element.17), channel_id=1, source_target_pairs={{0,3},{1,0},{2,1},{3,2},{4,7},{5,4},{6,5},{7,6},{8,11},{9,8},{10,9... | collective-permute-start | bytes 786440 | tf_op jit(solution)/shard_map/ppermute | solution.py:261
  22.2 3.4 %collective-permute-start.10 = (f32[264,512]{1,0:T(8,128)S(1)}, f32[264,512]{1,0:T(8,128)S(1)}, u32[]{:S(2)}, u32[]{:S(2)}) collective-permute-start(f32[264,512]{1,0:T(8,128)S(1)} %dynamic-slice_select_fusion), channel_id=1, source_target_pairs={{0,8},{4,12},{8,16},{12,20},{16,24},{20,28},{24,32},{28,36},{32,40... | collective-permute-start | bytes 1622024 | tf_op jit(solution)/shard_map/ppermute | solution.py:295
  25.6 4.9 %collective-permute-done.2 = f32[512,128]{1,0:T(8,128)S(1)} collective-permute-done((f32[512,128]{1,0:T(8,128)S(1)}, f32[512,128]{1,0:T(8,128)S(1)}, u32[]{:S(2)}, u32[]{:S(2)}) %collective-permute-start.2) | collective-permute-done | bytes 262176 | tf_op jit(solution)/shard_map/ppermute | solution.py:261
  30.5 0.6 collective-permute-done.3
  31.2 5.2 %collective-permute-start.5 = (f32[512,128]{1,0:T(8,128)S(1)}, f32[512,128]{1,0:T(8,128)S(1)}, u32[]{:S(2)}, u32[]{:S(2)}) collective-permute-start(f32[512,128]{1,0:T(8,128)S(1)} %bitcast_add_fusion.1.earlier.own), channel_id=1, source_target_pairs={{0,12},{4,8},{8,20},{12,16},{16,28},{20,24},{24,36},{28,32},{32,44... | collective-permute-start | bytes 786440 | tf_op jit(solution)/shard_map/ppermute | solution.py:303
  36.4 1.3 %collective-permute-start.6 = (f32[512,128]{1,0:T(8,128)S(1)}, f32[512,128]{1,0:T(8,128)S(1)}, u32[]{:S(2)}, u32[]{:S(2)}) collective-permute-start(f32[512,128]{1,0:T(8,128)S(1)} %bitcast_add_fusion.1.earlier.own), channel_id=1, source_target_pairs={{4,16},{12,24},{20,32},{28,40},{36,48},{44,56},{52,64},{60,72},{68... | collective-permute-start | bytes 786440 | tf_op jit(solution)/shard_map/ppermute | solution.py:304
  37.7 1.0 %collective-permute-done.10.array = f32[264,512]{1,0:T(8,128)S(1)} collective-permute-done((f32[264,512]{1,0:T(8,128)S(1)}, f32[264,512]{1,0:T(8,128)S(1)}, u32[]{:S(2)}, u32[]{:S(2)}) %collective-permute-start.10) | collective-permute-done | bytes 540704 | tf_op jit(solution)/shard_map/ppermute | solution.py:295
  38.8 2.5 %collective-permute-start.11 = (f32[264,512]{1,0:T(8,128)S(1)}, f32[264,512]{1,0:T(8,128)}, u32[]{:S(2)}, u32[]{:S(2)}) collective-permute-start(f32[264,512]{1,0:T(8,128)S(1)} %get-tuple-element.19.near), channel_id=1, source_target_pairs={{0,4},{4,0},{8,12},{12,8},{16,20},{20,16},{24,28},{28,24},{32,36},... | collective-permute-start | bytes 1622024 | tf_op jit(solution)/shard_map/ppermute | solution.py:316
  41.5 1.9 %copy-done.3 = f32[1,1,1536,512]{3,2,1,0:T(8,128)S(1)} copy-done((f32[1,1,1536,512]{3,2,1,0:T(8,128)S(1)}, f32[1,1,1536,512]{3,2,1,0:T(8,128)}, u32[]{:S(2)}) %copy-start.3) | copy-done | bytes 3145752
  43.4 1.2 %lower_prepare.1 = (bf16[1536,512]{1,0:T(8,128)(2,1)S(1)}, bf16[1536,512]{1,0:T(8,128)(2,1)S(1)}) custom-call(s32[48]{0:T(128)S(1)} %reshape.8.pattern, f32[1,1,1536,512]{3,2,1,0:T(8,128)S(1)} %copy-done.3), custom_call_target="tpu_custom_call" | custom-call | flops 1048576 | bytes 65536 | tf_op jit(solution)/shard_map/lower_prepare/pallas_call | solution.py:48
  44.8 0.9 %collective-permute-done.5.array = f32[512,128]{1,0:T(8,128)S(1)} collective-permute-done((f32[512,128]{1,0:T(8,128)S(1)}, f32[512,128]{1,0:T(8,128)S(1)}, u32[]{:S(2)}, u32[]{:S(2)}) %collective-permute-start.5) | collective-permute-done | bytes 262176 | tf_op jit(solution)/shard_map/ppermute | solution.py:303
  45.6 6.4 %collective-permute-done.6.earlier.far = f32[512,128]{1,0:T(8,128)S(1)} collective-permute-done((f32[512,128]{1,0:T(8,128)S(1)}, f32[512,128]{1,0:T(8,128)S(1)}, u32[]{:S(2)}, u32[]{:S(2)}) %collective-permute-start.6) | collective-permute-done | bytes 262176 | tf_op jit(solution)/shard_map/ppermute | solution.py:304
  52.0 0.7 slice.13
  53.0 2.2 %copy-done = f32[2048,512]{1,0:T(8,128)S(1)} copy-done((f32[2048,512]{1,0:T(8,128)S(1)}, f32[2048,512]{1,0:T(8,128)}, u32[]{:S(2)}) %copy-start) | copy-done | bytes 4194328
  55.2 5.7 %lower_cross.1.p_ref = f32[512,512]{1,0:T(8,128)S(1)} custom-call(s32[2]{0:T(128)S(1)} %pad_add_fusion.1.code, s32[3]{0:T(128)S(1)} %pad_add_fusion.where, s32[8]{0:T(128)S(1)} %select_reduce_fusion.far_tiles, f32[528,512]{1,0:T(8,128)S(1)} %upper_rows.1.block.own, f32[528,512]{1,0:T(8,128)S(1)} %collective-permute-done.8.other, ...), custom_call_target="tpu_custom_call" | custom-call | flops 1048576 | bytes 65536 | tf_op jit(solution)/shard_map/lower_cross/pallas_call | solution.py:48
  60.9 1.6 %lower_sum.1 = (f32[512,128]{1,0:T(8,128)S(1)}, f32[512,128]{1,0:T(8,128)S(1)}, f32[512,128]{1,0:T(8,128)S(1)}, f32[512,128]{1,0:T(8,128)S(1)}) custom-call(s32[2]{0:T(128)S(1)} %pad_add_fusion.1.code, s32[3]{0:T(128)S(1)} %pad_add_fusion.where, f32[512,128]{1,0:T(8,128)S(1)} %bitcast_add_fusion.1.earlier.own, f32[512,128]{1,0:T(8,128)S(1)} %collective-permute-done.4.even, ...), custom_call_target="tpu_custom_call" | custom-call | flops 1048576 | bytes 65536 | tf_op jit(solution)/shard_map/lower_sum/pallas_call | solution.py:48
  62.5 1.2 %collective-permute-start.12 = (f32[512,128]{1,0:T(8,128)S(1)}, f32[512,128]{1,0:T(8,128)S(1)}, u32[]{:S(2)}, u32[]{:S(2)}) collective-permute-start(f32[512,128]{1,0:T(8,128)S(1)} %get-tuple-element.23), channel_id=1, source_target_pairs={{0,1},{1,2},{2,3},{3,0},{4,5},{5,6},{6,7},{7,4},{8,9},{9,10},{10,1... | collective-permute-start | bytes 786440 | tf_op jit(solution)/shard_map/ppermute | solution.py:261
  63.7 3.4 %collective-permute-start.13 = (f32[512,128]{1,0:T(8,128)S(1)}, f32[512,128]{1,0:T(8,128)S(1)}, u32[]{:S(2)}, u32[]{:S(2)}) collective-permute-start(f32[512,128]{1,0:T(8,128)S(1)} %get-tuple-element.24), channel_id=1, source_target_pairs={{0,2},{1,3},{2,0},{3,1},{4,6},{5,7},{6,4},{7,5},{8,10},{9,11},{10,... | collective-permute-start | bytes 786440 | tf_op jit(solution)/shard_map/ppermute | solution.py:261
  67.1 1.4 %collective-permute-start.14 = (f32[512,128]{1,0:T(8,128)S(1)}, f32[512,128]{1,0:T(8,128)S(1)}, u32[]{:S(2)}, u32[]{:S(2)}) collective-permute-start(f32[512,128]{1,0:T(8,128)S(1)} %get-tuple-element.25), channel_id=1, source_target_pairs={{0,3},{1,0},{2,1},{3,2},{4,7},{5,4},{6,5},{7,6},{8,11},{9,8},{10,9... | collective-permute-start | bytes 786440 | tf_op jit(solution)/shard_map/ppermute | solution.py:261
  68.5 4.1 %collective-permute-done.12 = f32[512,128]{1,0:T(8,128)S(1)} collective-permute-done((f32[512,128]{1,0:T(8,128)S(1)}, f32[512,128]{1,0:T(8,128)S(1)}, u32[]{:S(2)}, u32[]{:S(2)}) %collective-permute-start.12) | collective-permute-done | bytes 262176 | tf_op jit(solution)/shard_map/ppermute | solution.py:261
  72.6 6.8 %collective-permute-done.13 = f32[512,128]{1,0:T(8,128)S(1)} collective-permute-done((f32[512,128]{1,0:T(8,128)S(1)}, f32[512,128]{1,0:T(8,128)S(1)}, u32[]{:S(2)}, u32[]{:S(2)}) %collective-permute-start.13) | collective-permute-done | bytes 262176 | tf_op jit(solution)/shard_map/ppermute | solution.py:261
  79.4 0.8 bitcast_add_fusion
  (42 shorter events, 1.0 us)
Async XLA Ops:
  0.6 1.5 %collective-permute-start = (s32[1]{0:T(128)}, s32[1]{0:T(128)}, u32[]{:S(2)}, u32[]{:S(2)}) collective-permute-start(s32[1]{0:T(128)} %param.13), channel_id=1, source_target_pairs={{0,4},{4,0},{8,12},{12,8},{16,20},{20,16},{24,28},{28,24},{32,36},... | collective-permute-start | bytes 20 | tf_op jit(solution)/shard_map/ppermute | solution.py:278
  2.1 1.9 %copy-start.1 = (f32[1,1536,512]{2,1,0:T(8,128)S(1)}, f32[1,1536,512]{2,1,0:T(8,128)}, u32[]{:S(2)}) copy-start(f32[1,1536,512]{2,1,0:T(8,128)} %u_ref.4) | copy-start | bytes 9437188
  4.0 0.7 copy-start.5
  4.7 7.7 %copy-start.6 = (s32[1,12]{1,0:T(1,128)S(1)}, s32[1,12]{1,0:T(1,128)}, u32[]{:S(2)}) copy-start(s32[1,12]{1,0:T(1,128)} %anc.3) | copy-start | bytes 148
  10.1 12.0 %collective-permute-start.8 = (f32[528,512]{1,0:T(8,128)S(1)}, f32[528,512]{1,0:T(8,128)S(1)}, u32[]{:S(2)}, u32[]{:S(2)}) collective-permute-start(f32[528,512]{1,0:T(8,128)S(1)} %upper_rows.1.block.own), channel_id=1, source_target_pairs={{0,4},{4,0},{8,12},{12,8},{16,20},{20,16},{24,28},{28,24},{32,36},... | collective-permute-start | bytes 3244040 | tf_op jit(solution)/shard_map/ppermute | solution.py:288
  10.4 41.6 %collective-permute-start.9 = (f32[528,512]{1,0:T(8,128)S(1)}, f32[528,512]{1,0:T(8,128)}, u32[]{:S(2)}, u32[]{:S(2)}) collective-permute-start(f32[528,512]{1,0:T(8,128)S(1)} %upper_rows.1.block.own), channel_id=1, source_target_pairs={{4,16},{12,24},{20,32},{28,40},{36,48},{44,56},{52,64},{60,72},{68... | collective-permute-start | bytes 3244040 | tf_op jit(solution)/shard_map/ppermute | solution.py:296
  12.3 1.9 %copy-start.2 = (f32[1,1536,512]{2,1,0:T(8,128)S(1)}, f32[1,1536,512]{2,1,0:T(8,128)}, u32[]{:S(2)}) copy-start(f32[1,1536,512]{2,1,0:T(8,128)} %u_ref.4) | copy-start | bytes 9437188
  16.2 15.0 %copy-start.7 = (f32[1,512,128]{2,1,0:T(8,128)S(1)}, f32[1,512,128]{2,1,0:T(8,128)}, u32[]{:S(2)}) copy-start(f32[1,512,128]{2,1,0:T(8,128)} %param.12) | copy-start | bytes 786436
  16.2 9.4 %collective-permute-start.1 = (f32[512,128]{1,0:T(8,128)S(1)}, f32[512,128]{1,0:T(8,128)S(1)}, u32[]{:S(2)}, u32[]{:S(2)}) collective-permute-start(f32[512,128]{1,0:T(8,128)S(1)} %get-tuple-element.15), channel_id=1, source_target_pairs={{0,1},{1,2},{2,3},{3,0},{4,5},{5,6},{6,7},{7,4},{8,9},{9,10},{10,1... | collective-permute-start | bytes 786440 | tf_op jit(solution)/shard_map/ppermute | solution.py:261
  17.8 12.7 %collective-permute-start.2 = (f32[512,128]{1,0:T(8,128)S(1)}, f32[512,128]{1,0:T(8,128)S(1)}, u32[]{:S(2)}, u32[]{:S(2)}) collective-permute-start(f32[512,128]{1,0:T(8,128)S(1)} %get-tuple-element.16), channel_id=1, source_target_pairs={{0,2},{1,3},{2,0},{3,1},{4,6},{5,7},{6,4},{7,5},{8,10},{9,11},{10,... | collective-permute-start | bytes 786440 | tf_op jit(solution)/shard_map/ppermute | solution.py:261
  20.7 10.4 %collective-permute-start.3 = (f32[512,128]{1,0:T(8,128)S(1)}, f32[512,128]{1,0:T(8,128)S(1)}, u32[]{:S(2)}, u32[]{:S(2)}) collective-permute-start(f32[512,128]{1,0:T(8,128)S(1)} %get-tuple-element.17), channel_id=1, source_target_pairs={{0,3},{1,0},{2,1},{3,2},{4,7},{5,4},{6,5},{7,6},{8,11},{9,8},{10,9... | collective-permute-start | bytes 786440 | tf_op jit(solution)/shard_map/ppermute | solution.py:261
  22.2 16.5 %collective-permute-start.10 = (f32[264,512]{1,0:T(8,128)S(1)}, f32[264,512]{1,0:T(8,128)S(1)}, u32[]{:S(2)}, u32[]{:S(2)}) collective-permute-start(f32[264,512]{1,0:T(8,128)S(1)} %dynamic-slice_select_fusion), channel_id=1, source_target_pairs={{0,8},{4,12},{8,16},{12,20},{16,24},{20,28},{24,32},{28,36},{32,40... | collective-permute-start | bytes 1622024 | tf_op jit(solution)/shard_map/ppermute | solution.py:295
  31.1 10.2 %copy-start.9 = (s32[1,1,12,4]{2,3,1,0:T(4,128)S(1)}, s32[1,1,12,4]{2,3,1,0:T(4,128)}, u32[]{:S(2)}) copy-start(s32[1,1,12,4]{2,3,1,0:T(4,128)} %param.15) | copy-start | bytes 580
  31.2 29.7 %copy-start.4 = (f32[512,128]{1,0:T(8,128)}, f32[512,128]{1,0:T(8,128)S(1)}, u32[]{:S(2)}) copy-start(f32[512,128]{1,0:T(8,128)S(1)} %bitcast_add_fusion.1.earlier.own) | copy-start | bytes 786436
  31.2 14.4 %collective-permute-start.5 = (f32[512,128]{1,0:T(8,128)S(1)}, f32[512,128]{1,0:T(8,128)S(1)}, u32[]{:S(2)}, u32[]{:S(2)}) collective-permute-start(f32[512,128]{1,0:T(8,128)S(1)} %bitcast_add_fusion.1.earlier.own), channel_id=1, source_target_pairs={{0,12},{4,8},{8,20},{12,16},{16,28},{20,24},{24,36},{28,32},{32,44... | collective-permute-start | bytes 786440 | tf_op jit(solution)/shard_map/ppermute | solution.py:303
  36.4 15.6 %collective-permute-start.6 = (f32[512,128]{1,0:T(8,128)S(1)}, f32[512,128]{1,0:T(8,128)S(1)}, u32[]{:S(2)}, u32[]{:S(2)}) collective-permute-start(f32[512,128]{1,0:T(8,128)S(1)} %bitcast_add_fusion.1.earlier.own), channel_id=1, source_target_pairs={{4,16},{12,24},{20,32},{28,40},{36,48},{44,56},{52,64},{60,72},{68... | collective-permute-start | bytes 786440 | tf_op jit(solution)/shard_map/ppermute | solution.py:304
  38.8 14.2 %collective-permute-start.11 = (f32[264,512]{1,0:T(8,128)S(1)}, f32[264,512]{1,0:T(8,128)}, u32[]{:S(2)}, u32[]{:S(2)}) collective-permute-start(f32[264,512]{1,0:T(8,128)S(1)} %get-tuple-element.19.near), channel_id=1, source_target_pairs={{0,4},{4,0},{8,12},{12,8},{16,20},{20,16},{24,28},{28,24},{32,36},... | collective-permute-start | bytes 1622024 | tf_op jit(solution)/shard_map/ppermute | solution.py:316
  41.5 1.9 %copy-start.3 = (f32[1,1,1536,512]{3,2,1,0:T(8,128)S(1)}, f32[1,1,1536,512]{3,2,1,0:T(8,128)}, u32[]{:S(2)}) copy-start(f32[1,1,1536,512]{3,2,1,0:T(8,128)} %u_ref.5) | copy-start | bytes 9437188
  43.4 9.4 %copy-start.10 = (s32[1,1,8]{2,1,0:T(1,128)S(1)}, s32[1,1,8]{2,1,0:T(1,128)}, u32[]{:S(2)}) copy-start(s32[1,1,8]{2,1,0:T(1,128)} %param.14) | copy-start | bytes 100
  44.6 16.2 %collective-permute-start.4 = (f32[512,128]{1,0:T(8,128)S(1)}, f32[512,128]{1,0:T(8,128)S(1)}, u32[]{:S(2)}, u32[]{:S(2)}) collective-permute-start(f32[512,128]{1,0:T(8,128)S(1)} %bitcast_add_fusion.1.earlier.own), channel_id=1, source_target_pairs={{0,4},{4,0},{8,12},{12,8},{16,20},{20,16},{24,28},{28,24},{32,36},... | collective-permute-start | bytes 786440 | tf_op jit(solution)/shard_map/ppermute | solution.py:332
  52.0 8.8 %collective-permute-start.7 = (f32[512,128]{1,0:T(8,128)S(1)}, f32[512,128]{1,0:T(8,128)S(1)}, u32[]{:S(2)}, u32[]{:S(2)}) collective-permute-start(f32[512,128]{1,0:T(8,128)S(1)} %after.2.near), channel_id=1, source_target_pairs={{0,4},{4,0},{8,12},{12,8},{16,20},{20,16},{24,28},{28,24},{32,36},... | collective-permute-start | bytes 786440 | tf_op jit(solution)/shard_map/ppermute | solution.py:331
  53.0 2.2 %copy-start = (f32[2048,512]{1,0:T(8,128)S(1)}, f32[2048,512]{1,0:T(8,128)}, u32[]{:S(2)}) copy-start(f32[2048,512]{1,0:T(8,128)} %refs_7_.1) | copy-start | bytes 12582916
  60.8 18.6 %copy-start.8 = (f32[1,1,512,128]{3,2,1,0:T(8,128)S(1)}, f32[1,1,512,128]{3,2,1,0:T(8,128)}, u32[]{:S(2)}) copy-start(f32[1,1,512,128]{3,2,1,0:T(8,128)} %param.17) | copy-start | bytes 786436
  62.5 10.1 %collective-permute-start.12 = (f32[512,128]{1,0:T(8,128)S(1)}, f32[512,128]{1,0:T(8,128)S(1)}, u32[]{:S(2)}, u32[]{:S(2)}) collective-permute-start(f32[512,128]{1,0:T(8,128)S(1)} %get-tuple-element.23), channel_id=1, source_target_pairs={{0,1},{1,2},{2,3},{3,0},{4,5},{5,6},{6,7},{7,4},{8,9},{9,10},{10,1... | collective-permute-start | bytes 786440 | tf_op jit(solution)/shard_map/ppermute | solution.py:261
  63.7 15.7 %collective-permute-start.13 = (f32[512,128]{1,0:T(8,128)S(1)}, f32[512,128]{1,0:T(8,128)S(1)}, u32[]{:S(2)}, u32[]{:S(2)}) collective-permute-start(f32[512,128]{1,0:T(8,128)S(1)} %get-tuple-element.24), channel_id=1, source_target_pairs={{0,2},{1,3},{2,0},{3,1},{4,6},{5,7},{6,4},{7,5},{8,10},{9,11},{10,... | collective-permute-start | bytes 786440 | tf_op jit(solution)/shard_map/ppermute | solution.py:261
  67.1 12.3 %collective-permute-start.14 = (f32[512,128]{1,0:T(8,128)S(1)}, f32[512,128]{1,0:T(8,128)S(1)}, u32[]{:S(2)}, u32[]{:S(2)}) collective-permute-start(f32[512,128]{1,0:T(8,128)S(1)} %get-tuple-element.25), channel_id=1, source_target_pairs={{0,3},{1,0},{2,1},{3,2},{4,7},{5,4},{6,5},{7,6},{8,11},{9,8},{10,9... | collective-permute-start | bytes 786440 | tf_op jit(solution)/shard_map/ppermute | solution.py:261

commit v5 on v4

--- a/solution.py
+++ b/solution.py
@@ -259,7 +259,7 @@
 def to_owners(slabs, count):
     ways = [[(i, (i + r) % count) for i in range(count)] for r in range(count)]
     arrived = [lax.ppermute(slabs[r], "tile", ways[r]) for r in (2, 1, 3)]
-    return slabs[0], arrived[1], arrived[0], arrived[2]
+    return slabs[0], arrived[0], arrived[1], arrived[2]
 
 
 def body(top, anc_a, u_a, dinv_a, parent, sel_b, pattern, u_b, dinv_b):

time: 80.7 us -> 80.5 us (level)
  waiting for transfers between devices: 25.4 us -> 23.6 us
  starting transfers between devices: 26 us -> 27.3 us
    ppermute x6, waiting for transfers between devices: 16.5 us -> 14.9 us  [to_owners(): arrived = [lax.ppermute(slabs[r], 'tile', ways[r]) for r in (2, 1, 3)]]
    ppermute x1, starting transfers between devices: 2.47 us -> 3.38 us  [body(): swapped = lax.ppermute(near, 'leaf', swap)]
  transfers between devices with their start and end apart: 15 -> 15, of which waited for: 8 -> 7; matrix products, arithmetic and copies ran while one was open for 2% -> 2% of each run, Pallas kernels for 11% -> 11%
where the time goes in v5:
time: 80.5 us; the launch traced here: 79.7 us
  starting transfers between devices  27.3 us (34%)
  waiting for transfers between devices  23.6 us (29%)
  Pallas kernels  15.9 us (20%)
  local copies, waits for them, and re-layouts  9.44 us (12%)
  between operations  2.12 us (3%)
  other arithmetic  1.29 us (2%)
    pallas_call x5, Pallas kernels, call(): pl.pallas_call(kernel, grid_spec=pltpu.PrefetchScalarGridSpec(num_scalar_...  15.9 us
    ppermute x6, waiting for transfers between devices, to_owners(): arrived = [lax.ppermute(slabs[r], 'tile', ways[r]) for r in (2, 1, 3)]  14.9 us
    ppermute x6, starting transfers between devices, to_owners(): arrived = [lax.ppermute(slabs[r], 'tile', ways[r]) for r in (2, 1, 3)]  12.6 us
    unnamed x23, local copies, waits for them, and re-layouts  8.62 us
    ppermute x1, waiting for transfers between devices, body(): far_s = lax.ppermute(sigma_a, 'leaf', odd_on)  6.86 us
    ppermute x1, starting transfers between devices, body(): near_s = lax.ppermute(sigma_a, 'leaf', crossing)  4.79 us
    ppermute x1, starting transfers between devices, body(): near = lax.ppermute(latest, 'leaf', next_chip)  3.41 us
    ppermute x1, starting transfers between devices, body(): swapped = lax.ppermute(near, 'leaf', swap)  3.38 us
  transfers between devices with their start and end apart: 15, of which 7 were waited for; matrix products, arithmetic and copies ran while one was open for 2% of the time, Pallas kernels for 11%

profile of v5, /device:TPU:194, one launch (start us, length us, event | category | flops | bytes accessed | tf_op | source)
XLA Modules:
  0.0 79.7 jit_solution(1609688556111882753)
XLA Ops:
  1.5 0.6 collective-permute-done.others_parent
  2.1 1.9 %copy-done.1 = f32[1,1536,512]{2,1,0:T(8,128)S(1)} copy-done((f32[1,1536,512]{2,1,0:T(8,128)S(1)}, f32[1,1536,512]{2,1,0:T(8,128)}, u32[]{:S(2)}) %copy-start.1) | copy-done | bytes 3145752
  4.0 0.7 copy-done.5
  4.7 5.5 %upper_rows.1.block.own = f32[528,512]{1,0:T(8,128)S(1)} custom-call(s32[1,12]{1,0:T(1,128)S(1)} %copy-done.5, s32[1]{0:T(128)} %copy.20.parent, s32[1]{0:T(128)} %collective-permute-done.others_parent, s32[3]{0:T(128)S(1)} %pad_add_fusion.where, f32[2048,512]{1,0:T(8,128)} %refs_7_.1, f32[1,1536,512]{2,1,0:T(8,128)S(1)} %copy-done.1), custom_call_target="tpu_custom_call" | custom-call | flops 1048576 | bytes 65536 | tf_op jit(solution)/shard_map/upper_rows/pallas_call | solution.py:48
  10.1 0.3 collective-permute-start.8
  10.4 1.3 %collective-permute-start.9 = (f32[528,512]{1,0:T(8,128)S(1)}, f32[528,512]{1,0:T(8,128)}, u32[]{:S(2)}, u32[]{:S(2)}) collective-permute-start(f32[528,512]{1,0:T(8,128)S(1)} %upper_rows.1.block.own), channel_id=1, source_target_pairs={{4,16},{12,24},{20,32},{28,40},{36,48},{44,56},{52,64},{60,72},{68... | collective-permute-start | bytes 3244040 | tf_op jit(solution)/shard_map/ppermute | solution.py:296
  12.3 1.9 %copy-done.2 = f32[1,1536,512]{2,1,0:T(8,128)S(1)} copy-done((f32[1,1536,512]{2,1,0:T(8,128)S(1)}, f32[1,1536,512]{2,1,0:T(8,128)}, u32[]{:S(2)}) %copy-start.2) | copy-done | bytes 3145752
  14.2 1.9 %upper_sum.1 = (f32[512,128]{1,0:T(8,128)S(1)}, f32[512,128]{1,0:T(8,128)S(1)}, f32[512,128]{1,0:T(8,128)S(1)}, f32[512,128]{1,0:T(8,128)S(1)}) custom-call(s32[1,12]{1,0:T(1,128)S(1)} %copy-done.6, s32[3]{0:T(128)S(1)} %pad_add_fusion.where, f32[528,512]{1,0:T(8,128)S(1)} %upper_rows.1.block.own, f32[1,1536,512]{2,1,0:T(8,128)S(1)} %copy-done.2), custom_call_target="tpu_custom_call" | custom-call | flops 1048576 | bytes 65536 | tf_op jit(solution)/shard_map/upper_sum/pallas_call | solution.py:48
  16.2 3.3 %collective-permute-start.1 = (f32[512,128]{1,0:T(8,128)S(1)}, f32[512,128]{1,0:T(8,128)S(1)}, u32[]{:S(2)}, u32[]{:S(2)}) collective-permute-start(f32[512,128]{1,0:T(8,128)S(1)} %get-tuple-element.15), channel_id=1, source_target_pairs={{0,2},{1,3},{2,0},{3,1},{4,6},{5,7},{6,4},{7,5},{8,10},{9,11},{10,... | collective-permute-start | bytes 786440 | tf_op jit(solution)/shard_map/ppermute | solution.py:261
  19.4 0.7 collective-permute-start.2
  20.1 2.5 %collective-permute-start.3 = (f32[512,128]{1,0:T(8,128)S(1)}, f32[512,128]{1,0:T(8,128)S(1)}, u32[]{:S(2)}, u32[]{:S(2)}) collective-permute-start(f32[512,128]{1,0:T(8,128)S(1)} %get-tuple-element.17), channel_id=1, source_target_pairs={{0,3},{1,0},{2,1},{3,2},{4,7},{5,4},{6,5},{7,6},{8,11},{9,8},{10,9... | collective-permute-start | bytes 786440 | tf_op jit(solution)/shard_map/ppermute | solution.py:261
  22.8 3.4 %collective-permute-start.10 = (f32[264,512]{1,0:T(8,128)S(1)}, f32[264,512]{1,0:T(8,128)S(1)}, u32[]{:S(2)}, u32[]{:S(2)}) collective-permute-start(f32[264,512]{1,0:T(8,128)S(1)} %dynamic-slice_select_fusion), channel_id=1, source_target_pairs={{0,8},{4,12},{8,16},{12,20},{16,24},{20,28},{24,32},{28,36},{32,40... | collective-permute-start | bytes 1622024 | tf_op jit(solution)/shard_map/ppermute | solution.py:295
  26.2 5.0 %collective-permute-done.2 = f32[512,128]{1,0:T(8,128)S(1)} collective-permute-done((f32[512,128]{1,0:T(8,128)S(1)}, f32[512,128]{1,0:T(8,128)S(1)}, u32[]{:S(2)}, u32[]{:S(2)}) %collective-permute-start.2) | collective-permute-done | bytes 262176 | tf_op jit(solution)/shard_map/ppermute | solution.py:261
  31.4 4.8 %collective-permute-start.5 = (f32[512,128]{1,0:T(8,128)S(1)}, f32[512,128]{1,0:T(8,128)S(1)}, u32[]{:S(2)}, u32[]{:S(2)}) collective-permute-start(f32[512,128]{1,0:T(8,128)S(1)} %bitcast_add_fusion.1.earlier.own), channel_id=1, source_target_pairs={{0,12},{4,8},{8,20},{12,16},{16,28},{20,24},{24,36},{28,32},{32,44... | collective-permute-start | bytes 786440 | tf_op jit(solution)/shard_map/ppermute | solution.py:303
  36.2 1.3 %collective-permute-start.6 = (f32[512,128]{1,0:T(8,128)S(1)}, f32[512,128]{1,0:T(8,128)S(1)}, u32[]{:S(2)}, u32[]{:S(2)}) collective-permute-start(f32[512,128]{1,0:T(8,128)S(1)} %bitcast_add_fusion.1.earlier.own), channel_id=1, source_target_pairs={{4,16},{12,24},{20,32},{28,40},{36,48},{44,56},{52,64},{60,72},{68... | collective-permute-start | bytes 786440 | tf_op jit(solution)/shard_map/ppermute | solution.py:304
  37.5 0.8 %collective-permute-done.10.array = f32[264,512]{1,0:T(8,128)S(1)} collective-permute-done((f32[264,512]{1,0:T(8,128)S(1)}, f32[264,512]{1,0:T(8,128)S(1)}, u32[]{:S(2)}, u32[]{:S(2)}) %collective-permute-start.10) | collective-permute-done | bytes 540704 | tf_op jit(solution)/shard_map/ppermute | solution.py:295
  38.3 3.4 %collective-permute-start.11 = (f32[264,512]{1,0:T(8,128)S(1)}, f32[264,512]{1,0:T(8,128)}, u32[]{:S(2)}, u32[]{:S(2)}) collective-permute-start(f32[264,512]{1,0:T(8,128)S(1)} %get-tuple-element.19.near), channel_id=1, source_target_pairs={{0,4},{4,0},{8,12},{12,8},{16,20},{20,16},{24,28},{28,24},{32,36},... | collective-permute-start | bytes 1622024 | tf_op jit(solution)/shard_map/ppermute | solution.py:316
  42.0 1.9 %copy-done.3 = f32[1,1,1536,512]{3,2,1,0:T(8,128)S(1)} copy-done((f32[1,1,1536,512]{3,2,1,0:T(8,128)S(1)}, f32[1,1,1536,512]{3,2,1,0:T(8,128)}, u32[]{:S(2)}) %copy-start.3) | copy-done | bytes 3145752
  43.9 1.2 %lower_prepare.1 = (bf16[1536,512]{1,0:T(8,128)(2,1)S(1)}, bf16[1536,512]{1,0:T(8,128)(2,1)S(1)}) custom-call(s32[48]{0:T(128)S(1)} %reshape.8.pattern, f32[1,1,1536,512]{3,2,1,0:T(8,128)S(1)} %copy-done.3), custom_call_target="tpu_custom_call" | custom-call | flops 1048576 | bytes 65536 | tf_op jit(solution)/shard_map/lower_prepare/pallas_call | solution.py:48
  45.2 0.4 collective-permute-done.5.array
  45.6 6.9 %collective-permute-done.6.earlier.far = f32[512,128]{1,0:T(8,128)S(1)} collective-permute-done((f32[512,128]{1,0:T(8,128)S(1)}, f32[512,128]{1,0:T(8,128)S(1)}, u32[]{:S(2)}, u32[]{:S(2)}) %collective-permute-start.6) | collective-permute-done | bytes 262176 | tf_op jit(solution)/shard_map/ppermute | solution.py:304
  52.5 0.7 slice.13
  53.2 0.2 select_reduce_fusion.far_tiles
  53.4 2.2 %copy-done = f32[2048,512]{1,0:T(8,128)S(1)} copy-done((f32[2048,512]{1,0:T(8,128)S(1)}, f32[2048,512]{1,0:T(8,128)}, u32[]{:S(2)}) %copy-start) | copy-done | bytes 4194328
  55.6 5.7 %lower_cross.1.p_ref = f32[512,512]{1,0:T(8,128)S(1)} custom-call(s32[2]{0:T(128)S(1)} %pad_add_fusion.1.code, s32[3]{0:T(128)S(1)} %pad_add_fusion.where, s32[8]{0:T(128)S(1)} %select_reduce_fusion.far_tiles, f32[528,512]{1,0:T(8,128)S(1)} %upper_rows.1.block.own, f32[528,512]{1,0:T(8,128)S(1)} %collective-permute-done.8.other, ...), custom_call_target="tpu_custom_call" | custom-call | flops 1048576 | bytes 65536 | tf_op jit(solution)/shard_map/lower_cross/pallas_call | solution.py:48
  61.3 1.6 %lower_sum.1 = (f32[512,128]{1,0:T(8,128)S(1)}, f32[512,128]{1,0:T(8,128)S(1)}, f32[512,128]{1,0:T(8,128)S(1)}, f32[512,128]{1,0:T(8,128)S(1)}) custom-call(s32[2]{0:T(128)S(1)} %pad_add_fusion.1.code, s32[3]{0:T(128)S(1)} %pad_add_fusion.where, f32[512,128]{1,0:T(8,128)S(1)} %bitcast_add_fusion.1.earlier.own, f32[512,128]{1,0:T(8,128)S(1)} %collective-permute-done.4.even, ...), custom_call_target="tpu_custom_call" | custom-call | flops 1048576 | bytes 65536 | tf_op jit(solution)/shard_map/lower_sum/pallas_call | solution.py:48
  63.0 2.9 %collective-permute-start.12 = (f32[512,128]{1,0:T(8,128)S(1)}, f32[512,128]{1,0:T(8,128)S(1)}, u32[]{:S(2)}, u32[]{:S(2)}) collective-permute-start(f32[512,128]{1,0:T(8,128)S(1)} %get-tuple-element.23), channel_id=1, source_target_pairs={{0,2},{1,3},{2,0},{3,1},{4,6},{5,7},{6,4},{7,5},{8,10},{9,11},{10,... | collective-permute-start | bytes 786440 | tf_op jit(solution)/shard_map/ppermute | solution.py:261
  65.8 0.6 collective-permute-start.13
  66.5 2.6 %collective-permute-start.14 = (f32[512,128]{1,0:T(8,128)S(1)}, f32[512,128]{1,0:T(8,128)S(1)}, u32[]{:S(2)}, u32[]{:S(2)}) collective-permute-start(f32[512,128]{1,0:T(8,128)S(1)} %get-tuple-element.25), channel_id=1, source_target_pairs={{0,3},{1,0},{2,1},{3,2},{4,7},{5,4},{6,5},{7,6},{8,11},{9,8},{10,9... | collective-permute-start | bytes 786440 | tf_op jit(solution)/shard_map/ppermute | solution.py:261
  69.1 4.6 %collective-permute-done.12 = f32[512,128]{1,0:T(8,128)S(1)} collective-permute-done((f32[512,128]{1,0:T(8,128)S(1)}, f32[512,128]{1,0:T(8,128)S(1)}, u32[]{:S(2)}, u32[]{:S(2)}) %collective-permute-start.12) | collective-permute-done | bytes 262176 | tf_op jit(solution)/shard_map/ppermute | solution.py:261
  73.7 5.2 %collective-permute-done.13 = f32[512,128]{1,0:T(8,128)S(1)} collective-permute-done((f32[512,128]{1,0:T(8,128)S(1)}, f32[512,128]{1,0:T(8,128)S(1)}, u32[]{:S(2)}, u32[]{:S(2)}) %collective-permute-start.13) | collective-permute-done | bytes 262176 | tf_op jit(solution)/shard_map/ppermute | solution.py:261
  78.9 0.8 bitcast_add_fusion
  (42 shorter events, 0.8 us)
Async XLA Ops:
  0.6 1.5 %collective-permute-start = (s32[1]{0:T(128)}, s32[1]{0:T(128)}, u32[]{:S(2)}, u32[]{:S(2)}) collective-permute-start(s32[1]{0:T(128)} %param.13), channel_id=1, source_target_pairs={{0,4},{4,0},{8,12},{12,8},{16,20},{20,16},{24,28},{28,24},{32,36},... | collective-permute-start | bytes 20 | tf_op jit(solution)/shard_map/ppermute | solution.py:278
  2.1 1.9 %copy-start.1 = (f32[1,1536,512]{2,1,0:T(8,128)S(1)}, f32[1,1536,512]{2,1,0:T(8,128)}, u32[]{:S(2)}) copy-start(f32[1,1536,512]{2,1,0:T(8,128)} %u_ref.4) | copy-start | bytes 9437188
  4.0 0.7 copy-start.5
  4.7 7.7 %copy-start.6 = (s32[1,12]{1,0:T(1,128)S(1)}, s32[1,12]{1,0:T(1,128)}, u32[]{:S(2)}) copy-start(s32[1,12]{1,0:T(1,128)} %anc.3) | copy-start | bytes 148
  10.1 12.6 %collective-permute-start.8 = (f32[528,512]{1,0:T(8,128)S(1)}, f32[528,512]{1,0:T(8,128)S(1)}, u32[]{:S(2)}, u32[]{:S(2)}) collective-permute-start(f32[528,512]{1,0:T(8,128)S(1)} %upper_rows.1.block.own), channel_id=1, source_target_pairs={{0,4},{4,0},{8,12},{12,8},{16,20},{20,16},{24,28},{28,24},{32,36},... | collective-permute-start | bytes 3244040 | tf_op jit(solution)/shard_map/ppermute | solution.py:288
  10.4 42.1 %collective-permute-start.9 = (f32[528,512]{1,0:T(8,128)S(1)}, f32[528,512]{1,0:T(8,128)}, u32[]{:S(2)}, u32[]{:S(2)}) collective-permute-start(f32[528,512]{1,0:T(8,128)S(1)} %upper_rows.1.block.own), channel_id=1, source_target_pairs={{4,16},{12,24},{20,32},{28,40},{36,48},{44,56},{52,64},{60,72},{68... | collective-permute-start | bytes 3244040 | tf_op jit(solution)/shard_map/ppermute | solution.py:296
  12.3 1.9 %copy-start.2 = (f32[1,1536,512]{2,1,0:T(8,128)S(1)}, f32[1,1536,512]{2,1,0:T(8,128)}, u32[]{:S(2)}) copy-start(f32[1,1536,512]{2,1,0:T(8,128)} %u_ref.4) | copy-start | bytes 9437188
  16.2 15.1 %copy-start.7 = (f32[1,512,128]{2,1,0:T(8,128)S(1)}, f32[1,512,128]{2,1,0:T(8,128)}, u32[]{:S(2)}) copy-start(f32[1,512,128]{2,1,0:T(8,128)} %param.12) | copy-start | bytes 786436
  16.2 10.0 %collective-permute-start.1 = (f32[512,128]{1,0:T(8,128)S(1)}, f32[512,128]{1,0:T(8,128)S(1)}, u32[]{:S(2)}, u32[]{:S(2)}) collective-permute-start(f32[512,128]{1,0:T(8,128)S(1)} %get-tuple-element.15), channel_id=1, source_target_pairs={{0,2},{1,3},{2,0},{3,1},{4,6},{5,7},{6,4},{7,5},{8,10},{9,11},{10,... | collective-permute-start | bytes 786440 | tf_op jit(solution)/shard_map/ppermute | solution.py:261
  19.4 11.8 %collective-permute-start.2 = (f32[512,128]{1,0:T(8,128)S(1)}, f32[512,128]{1,0:T(8,128)S(1)}, u32[]{:S(2)}, u32[]{:S(2)}) collective-permute-start(f32[512,128]{1,0:T(8,128)S(1)} %get-tuple-element.16), channel_id=1, source_target_pairs={{0,1},{1,2},{2,3},{3,0},{4,5},{5,6},{6,7},{7,4},{8,9},{9,10},{10,1... | collective-permute-start | bytes 786440 | tf_op jit(solution)/shard_map/ppermute | solution.py:261
  20.1 11.1 %collective-permute-start.3 = (f32[512,128]{1,0:T(8,128)S(1)}, f32[512,128]{1,0:T(8,128)S(1)}, u32[]{:S(2)}, u32[]{:S(2)}) collective-permute-start(f32[512,128]{1,0:T(8,128)S(1)} %get-tuple-element.17), channel_id=1, source_target_pairs={{0,3},{1,0},{2,1},{3,2},{4,7},{5,4},{6,5},{7,6},{8,11},{9,8},{10,9... | collective-permute-start | bytes 786440 | tf_op jit(solution)/shard_map/ppermute | solution.py:261
  22.8 15.5 %collective-permute-start.10 = (f32[264,512]{1,0:T(8,128)S(1)}, f32[264,512]{1,0:T(8,128)S(1)}, u32[]{:S(2)}, u32[]{:S(2)}) collective-permute-start(f32[264,512]{1,0:T(8,128)S(1)} %dynamic-slice_select_fusion), channel_id=1, source_target_pairs={{0,8},{4,12},{8,16},{12,20},{16,24},{20,28},{24,32},{28,36},{32,40... | collective-permute-start | bytes 1622024 | tf_op jit(solution)/shard_map/ppermute | solution.py:295
  31.3 10.5 %copy-start.9 = (s32[1,1,12,4]{2,3,1,0:T(4,128)S(1)}, s32[1,1,12,4]{2,3,1,0:T(4,128)}, u32[]{:S(2)}) copy-start(s32[1,1,12,4]{2,3,1,0:T(4,128)} %param.15) | copy-start | bytes 580
  31.4 30.0 %copy-start.4 = (f32[512,128]{1,0:T(8,128)}, f32[512,128]{1,0:T(8,128)S(1)}, u32[]{:S(2)}) copy-start(f32[512,128]{1,0:T(8,128)S(1)} %bitcast_add_fusion.1.earlier.own) | copy-start | bytes 786436
  31.4 14.3 %collective-permute-start.5 = (f32[512,128]{1,0:T(8,128)S(1)}, f32[512,128]{1,0:T(8,128)S(1)}, u32[]{:S(2)}, u32[]{:S(2)}) collective-permute-start(f32[512,128]{1,0:T(8,128)S(1)} %bitcast_add_fusion.1.earlier.own), channel_id=1, source_target_pairs={{0,12},{4,8},{8,20},{12,16},{16,28},{20,24},{24,36},{28,32},{32,44... | collective-permute-start | bytes 786440 | tf_op jit(solution)/shard_map/ppermute | solution.py:303
  36.2 16.3 %collective-permute-start.6 = (f32[512,128]{1,0:T(8,128)S(1)}, f32[512,128]{1,0:T(8,128)S(1)}, u32[]{:S(2)}, u32[]{:S(2)}) collective-permute-start(f32[512,128]{1,0:T(8,128)S(1)} %bitcast_add_fusion.1.earlier.own), channel_id=1, source_target_pairs={{4,16},{12,24},{20,32},{28,40},{36,48},{44,56},{52,64},{60,72},{68... | collective-permute-start | bytes 786440 | tf_op jit(solution)/shard_map/ppermute | solution.py:304
  38.3 15.1 %collective-permute-start.11 = (f32[264,512]{1,0:T(8,128)S(1)}, f32[264,512]{1,0:T(8,128)}, u32[]{:S(2)}, u32[]{:S(2)}) collective-permute-start(f32[264,512]{1,0:T(8,128)S(1)} %get-tuple-element.19.near), channel_id=1, source_target_pairs={{0,4},{4,0},{8,12},{12,8},{16,20},{20,16},{24,28},{28,24},{32,36},... | collective-permute-start | bytes 1622024 | tf_op jit(solution)/shard_map/ppermute | solution.py:316
  42.0 1.9 %copy-start.3 = (f32[1,1,1536,512]{3,2,1,0:T(8,128)S(1)}, f32[1,1,1536,512]{3,2,1,0:T(8,128)}, u32[]{:S(2)}) copy-start(f32[1,1,1536,512]{3,2,1,0:T(8,128)} %u_ref.5) | copy-start | bytes 9437188
  43.8 9.4 %copy-start.10 = (s32[1,1,8]{2,1,0:T(1,128)S(1)}, s32[1,1,8]{2,1,0:T(1,128)}, u32[]{:S(2)}) copy-start(s32[1,1,8]{2,1,0:T(1,128)} %param.14) | copy-start | bytes 100
  45.1 16.2 %collective-permute-start.4 = (f32[512,128]{1,0:T(8,128)S(1)}, f32[512,128]{1,0:T(8,128)S(1)}, u32[]{:S(2)}, u32[]{:S(2)}) collective-permute-start(f32[512,128]{1,0:T(8,128)S(1)} %bitcast_add_fusion.1.earlier.own), channel_id=1, source_target_pairs={{0,4},{4,0},{8,12},{12,8},{16,20},{20,16},{24,28},{28,24},{32,36},... | collective-permute-start | bytes 786440 | tf_op jit(solution)/shard_map/ppermute | solution.py:332
  52.5 8.8 %collective-permute-start.7 = (f32[512,128]{1,0:T(8,128)S(1)}, f32[512,128]{1,0:T(8,128)S(1)}, u32[]{:S(2)}, u32[]{:S(2)}) collective-permute-start(f32[512,128]{1,0:T(8,128)S(1)} %after.2.near), channel_id=1, source_target_pairs={{0,4},{4,0},{8,12},{12,8},{16,20},{20,16},{24,28},{28,24},{32,36},... | collective-permute-start | bytes 786440 | tf_op jit(solution)/shard_map/ppermute | solution.py:331
  53.4 2.2 %copy-start = (f32[2048,512]{1,0:T(8,128)S(1)}, f32[2048,512]{1,0:T(8,128)}, u32[]{:S(2)}) copy-start(f32[2048,512]{1,0:T(8,128)} %refs_7_.1) | copy-start | bytes 12582916
  61.3 17.6 %copy-start.8 = (f32[1,1,512,128]{3,2,1,0:T(8,128)S(1)}, f32[1,1,512,128]{3,2,1,0:T(8,128)}, u32[]{:S(2)}) copy-start(f32[1,1,512,128]{3,2,1,0:T(8,128)} %param.17) | copy-start | bytes 786436
  63.0 10.7 %collective-permute-start.12 = (f32[512,128]{1,0:T(8,128)S(1)}, f32[512,128]{1,0:T(8,128)S(1)}, u32[]{:S(2)}, u32[]{:S(2)}) collective-permute-start(f32[512,128]{1,0:T(8,128)S(1)} %get-tuple-element.23), channel_id=1, source_target_pairs={{0,2},{1,3},{2,0},{3,1},{4,6},{5,7},{6,4},{7,5},{8,10},{9,11},{10,... | collective-permute-start | bytes 786440 | tf_op jit(solution)/shard_map/ppermute | solution.py:261
  65.8 13.1 %collective-permute-start.13 = (f32[512,128]{1,0:T(8,128)S(1)}, f32[512,128]{1,0:T(8,128)S(1)}, u32[]{:S(2)}, u32[]{:S(2)}) collective-permute-start(f32[512,128]{1,0:T(8,128)S(1)} %get-tuple-element.24), channel_id=1, source_target_pairs={{0,1},{1,2},{2,3},{3,0},{4,5},{5,6},{6,7},{7,4},{8,9},{9,10},{10,1... | collective-permute-start | bytes 786440 | tf_op jit(solution)/shard_map/ppermute | solution.py:261
  66.5 12.4 %collective-permute-start.14 = (f32[512,128]{1,0:T(8,128)S(1)}, f32[512,128]{1,0:T(8,128)S(1)}, u32[]{:S(2)}, u32[]{:S(2)}) collective-permute-start(f32[512,128]{1,0:T(8,128)S(1)} %get-tuple-element.25), channel_id=1, source_target_pairs={{0,3},{1,0},{2,1},{3,2},{4,7},{5,4},{6,5},{7,6},{8,11},{9,8},{10,9... | collective-permute-start | bytes 786440 | tf_op jit(solution)/shard_map/ppermute | solution.py:261
